TPU v7x, 32 devices: a whole 2x2x4 slice. The times are simulated.
32 devices in a mesh: seq: 8 (over z, x), head: 4 (over y, core).
Axes of the slice: x: 2, y: 2, z: 4, core: 2. Of those that a mesh axis runs over, the one named last changes fastest.
Arguments:
- tokens: bfloat16 [2048, 5376], P('seq'), may hold values from -6 to 6
- q_weight: bfloat16 [5376, 2048], P('seq', 'head')
- k_weight: bfloat16 [5376, 1024], P('seq', 'head')
- v_weight: bfloat16 [5376, 1024], P('seq', 'head'), may hold values from -0.078125 to 0.078125
- q_gain: float32 [128], replicated, may hold values from 0.5 to 6
- k_gain: float32 [128], replicated, may hold values from 0.5 to 6
- windows: int32 [16], P('head'), may hold values from 512 to 1024, as said below
- token_weight: float32 [2048], P('seq'), may hold values from 0.3 to 6
- loss_mask: int32 [2048], P('seq'), may hold values from 0 to 1, as said below
- grad_attn: bfloat16 [2048, 2048], P('seq', 'head'), may hold values from -6 to 6
Outputs:
- attn: bfloat16 [2048, 2048], P('seq', 'head')
- grad_tokens: bfloat16 [2048, 5376], P('seq', 'head')
Inputs may be any that keep to these rules, and one draw needn't show every extreme that they name: `windows`: some head has a window of exactly 1024 keys and some head exactly 512. `loss_mask`: the first token always counts.
All inputs are finite; a program needn't handle non-finite values.
Results may differ from a plain program's by a relative error of at most 0.038.
The roundings to bfloat16 on the way count: a program that leaves them out, or rounds other values in their place, can miss the bound.
Values may be sent and summed in bfloat16 or wider, within the bound.
A program may use at most 128 MiB of HBM per device.

v0:
```python
import jax
import jax.numpy as jnp
from jax import lax
from jax.sharding import PartitionSpec as P

QPRE = 168
WINDOW = 1024


norm_eps = 1e-06


def passed_along(block, axis, distance):
    devices = range(lax.axis_size(axis))
    route = [(i - distance, i) for i in devices if i - distance in devices]
    return lax.ppermute(block, axis, route)


def rotate_table(positions, head_width):
    half_width = head_width // 2
    frequency = 10000.0 ** (-(jnp.arange(half_width, dtype=jnp.float32) * 2.0) / head_width)
    angles = positions.astype(jnp.float32)[:, None] * frequency[None, :]
    return (jnp.cos(angles)[:, None, :], jnp.sin(angles)[:, None, :])


def norm_rotate(linear, gain_vec, cosine, sine_table):
    mean_square = jnp.mean(linear * linear, axis=-1, keepdims=True)
    normed = linear * lax.rsqrt(mean_square + norm_eps) * gain_vec
    half_width = linear.shape[-1] // 2
    first_half = normed[..., :half_width]
    second_half = normed[..., half_width:]
    return jnp.concatenate(
        [
            first_half * cosine - second_half * sine_table,
            second_half * cosine + first_half * sine_table,
        ],
        axis=-1,
    )


def block_grad(queries, key_rows, value_rows, cotangent, query_pos, key_pos, windows, score_scale):
    tok_rows, q_heads, head_width = queries.shape
    kv_heads = key_rows.shape[1]
    group_size = q_heads // kv_heads
    query_grp = queries.reshape(tok_rows, kv_heads, group_size, head_width)
    cotan_grp = cotangent.reshape(tok_rows, kv_heads, group_size, head_width)
    scores = score_scale * jnp.einsum(
        "tgjd,sgd->gjts", query_grp, key_rows, preferred_element_type=jnp.float32
    )
    distance = query_pos[:, None] - key_pos[None, :]
    reach = windows.reshape(kv_heads, group_size)[:, :, None, None]
    allowed = (
        (distance[None, None] >= 0)
        & (distance[None, None] < reach)
        & (key_pos >= 0)[None, None, None, :]
    )
    masked = jnp.where(allowed, scores, jnp.float32(-1e30))
    row_peak = jnp.max(masked, axis=-1, keepdims=True)
    row_total = jnp.sum(
        jnp.where(allowed, jnp.exp(masked - row_peak), jnp.float32(0.0)), axis=-1, keepdims=True
    )
    logsum = row_peak + jnp.log(row_total)
    probability = jnp.where(allowed, jnp.exp(masked - logsum), jnp.float32(0.0))
    probs_b = probability.astype(jnp.bfloat16)
    attended = jnp.einsum(
        "gjts,sgd->tgjd", probs_b, value_rows, preferred_element_type=jnp.float32
    ).astype(jnp.bfloat16)
    row_delta = jnp.sum(cotan_grp.astype(jnp.float32) * attended.astype(jnp.float32), axis=-1)
    dprobs = jnp.einsum("tgjd,sgd->gjts", cotan_grp, value_rows, preferred_element_type=jnp.float32)
    dscore = (probability * (dprobs - jnp.transpose(row_delta, (1, 2, 0))[..., None])).astype(
        jnp.bfloat16
    )
    dquery = score_scale * jnp.einsum(
        "gjts,sgd->tgjd", dscore, key_rows, preferred_element_type=jnp.float32
    )
    key_grads = score_scale * jnp.einsum(
        "gjts,tgjd->sgd", dscore, query_grp, preferred_element_type=jnp.float32
    )
    dvalues = jnp.einsum("gjts,tgjd->sgd", probs_b, cotan_grp, preferred_element_type=jnp.float32)
    return (
        attended.reshape(tok_rows, q_heads * head_width),
        dquery.reshape(tok_rows, q_heads, head_width),
        key_grads,
        dvalues,
    )


def body(
    tokens,
    q_weight,
    k_weight,
    v_weight,
    q_gain,
    k_gain,
    windows,
    token_weight,
    loss_mask,
    grad_attn,
):
    tok_rows = tokens.shape[0]
    head_width = q_gain.shape[0]
    q_heads = q_weight.shape[1] // head_width
    kv_heads = k_weight.shape[1] // head_width
    pred_count = WINDOW // tok_rows
    key_span = (pred_count + 1) * tok_rows
    score_scale = QPRE ** (-0.5)
    first_row = lax.axis_index("seq") * tok_rows
    positions = first_row + jnp.arange(tok_rows, dtype=jnp.int32)
    key_pos = first_row - pred_count * tok_rows + jnp.arange(key_span, dtype=jnp.int32)
    kept_weight = token_weight * loss_mask.astype(jnp.float32)
    normalizer = lax.psum(jnp.sum(kept_weight), "seq")
    factor = kept_weight * (tok_rows * lax.axis_size("seq") / normalizer)
    cotangent = (
        (grad_attn.astype(jnp.float32) * factor[:, None])
        .astype(jnp.bfloat16)
        .reshape(tok_rows, q_heads, head_width)
    )
    row_pieces = (q_weight, k_weight, v_weight)
    contract = (((1,), (1,)), ((), ()))
    pieces_now = (
        lax.all_gather(row_pieces[0], "seq", axis=0, tiled=True),
        lax.all_gather(row_pieces[1], "seq", axis=0, tiled=True),
        lax.all_gather(row_pieces[2], "seq", axis=0, tiled=True),
    )
    q_linear, k_linear, v_linear = tuple(
        (jnp.dot(tokens, matrix, preferred_element_type=jnp.float32) for matrix in pieces_now)
    )
    q_linear = q_linear.reshape(tok_rows, q_heads, head_width)
    k_linear = k_linear.reshape(tok_rows, kv_heads, head_width)
    values = v_linear.astype(jnp.bfloat16)
    cosine, sine_table = rotate_table(positions, head_width)
    q_rot = norm_rotate(q_linear, q_gain, cosine, sine_table).astype(jnp.bfloat16)
    k_rot = norm_rotate(k_linear, k_gain, cosine, sine_table).astype(jnp.bfloat16)
    stacked = jnp.stack([k_rot.reshape(tok_rows, kv_heads * head_width), values])
    received = []
    for offset in range(1, pred_count + 1):
        received.append(passed_along(stacked, "seq", offset))
    extended = jnp.concatenate(received[::-1] + [stacked], axis=1)
    key_rows = extended[0].reshape(key_span, kv_heads, head_width)
    value_rows = extended[1].reshape(key_span, kv_heads, head_width)
    attended, dquery, key_grads, dvalues = block_grad(
        q_rot, key_rows, value_rows, cotangent, positions, key_pos, windows, score_scale
    )
    stacked_grads = jnp.stack(
        [
            key_grads.reshape(key_span, kv_heads * head_width),
            dvalues.reshape(key_span, kv_heads * head_width),
        ]
    )
    local_grads = stacked_grads[:, pred_count * tok_rows :]
    for offset in range(1, pred_count + 1):
        local_grads = local_grads + passed_along(
            stacked_grads[
                :, (pred_count - offset) * tok_rows : (pred_count - offset + 1) * tok_rows
            ].astype(jnp.bfloat16),
            "seq",
            -offset,
        ).astype(jnp.float32)
    key_total = local_grads[0].reshape(tok_rows, kv_heads, head_width)
    _, back_query = jax.vjp(
        lambda linear_in: norm_rotate(linear_in, q_gain, cosine, sine_table), q_linear
    )
    _, back_key = jax.vjp(
        lambda linear_in: norm_rotate(linear_in, k_gain, cosine, sine_table), k_linear
    )
    dq_lin = back_query(dquery)[0].astype(jnp.bfloat16).reshape(tok_rows, q_heads * head_width)
    dk_lin = back_key(key_total)[0].astype(jnp.bfloat16).reshape(tok_rows, kv_heads * head_width)
    dv_lin = local_grads[1].astype(jnp.bfloat16)
    joined_grad = jnp.concatenate([dq_lin, dk_lin, dv_lin], axis=1)
    joined_rows = jnp.concatenate([q_weight, k_weight, v_weight], axis=1)
    partial_grad = lax.dot_general(
        joined_grad,
        lax.all_gather(joined_rows, "seq", axis=0, tiled=True),
        contract,
        preferred_element_type=jnp.float32,
    )
    grad_tokens = lax.psum_scatter(
        partial_grad.astype(jnp.bfloat16), "head", scatter_dimension=1, tiled=True
    )
    return (attended, grad_tokens)


def solution(mesh):
    in_specs = (
        P("seq", None),
        P("seq", "head"),
        P("seq", "head"),
        P("seq", "head"),
        P(),
        P(),
        P("head"),
        P("seq"),
        P("seq"),
        P("seq", "head"),
    )
    out_specs = (P("seq", "head"), P("seq", "head"))
    return jax.shard_map(body, mesh=mesh, in_specs=in_specs, out_specs=out_specs, check_vma=False)
```

profile of v0, /device:TPU:18, one launch (start us, length us, event | category | flops | bytes accessed | tf_op | source)
XLA Modules:
  0.0 465.1 jit_solution(16645605638941714412)
XLA Ops:
  9.5 2.6 pad_maximum_fusion.1
  12.8 15.8 %psum.7 = f32[]{:T(128)} all-reduce(f32[]{:T(128)} %fusion.23), channel_id=1, replica_groups=mesh['seq'=8,'head'=4] {'seq'}, use_global_device_ids=true, to_apply=%region_5.6 | all-reduce | flops 1 | bytes 8 | tf_op jit(solution)/shard_map/psum | solution.py:111
  31.1 1.4 broadcast_subtract_fusion
  32.5 33.6 %all-gather.5.cloned.1.call-done = bf16[5376,256]{1,0:T(8,128)(2,1)} async-done(((bf16[672,256]{1,0:T(8,128)(2,1)}), bf16[5376,256]{1,0:T(8,128)(2,1)}) %all-gather.5.cloned.1.call-update) | async-done | bytes 2752528 | tf_op jit(solution)/shard_map/all_gather | solution.py:122
  66.1 3.0 multiply_reduce_fusion.4
  69.4 53.6 %all-gather.7.cloned.1.call-done = bf16[5376,256]{1,0:T(8,128)(2,1)} async-done(((bf16[672,256]{1,0:T(8,128)(2,1)}), bf16[5376,256]{1,0:T(8,128)(2,1)}) %all-gather.7.cloned.1.call-update) | async-done | bytes 2752528 | tf_op jit(solution)/shard_map/all_gather | solution.py:123
  123.0 2.7 fusion.5
  126.4 1.3 collective-permute-start
  127.7 1.3 collective-permute-start.1
  129.1 2.5 collective-permute-start.2
  133.7 2.4 collective-permute-start.3
  136.0 5.8 %collective-permute-done = bf16[2,256,256]{2,1,0:T(8,128)(2,1)} collective-permute-done((bf16[2,256,256]{2,1,0:T(8,128)(2,1)}, bf16[2,256,256]{2,1,0:T(8,128)(2,1)}, u32[]{:S(2)}, u32[]{:S(2)}) %collective-permute-start) | collective-permute-done | bytes 262176 | tf_op jit(solution)/shard_map/ppermute | solution.py:16
  142.8 28.4 %collective-permute-done.1 = bf16[2,256,256]{2,1,0:T(8,128)(2,1)} collective-permute-done((bf16[2,256,256]{2,1,0:T(8,128)(2,1)}, bf16[2,256,256]{2,1,0:T(8,128)(2,1)}, u32[]{:S(2)}, u32[]{:S(2)}) %collective-permute-start.1) | collective-permute-done | bytes 262176 | tf_op jit(solution)/shard_map/ppermute | solution.py:16
  172.2 9.4 %collective-permute-done.2 = bf16[2,256,256]{2,1,0:T(8,128)(2,1)} collective-permute-done((bf16[2,256,256]{2,1,0:T(8,128)(2,1)}, bf16[2,256,256]{2,1,0:T(8,128)(2,1)}, u32[]{:S(2)}, u32[]{:S(2)}) %collective-permute-start.2) | collective-permute-done | bytes 262176 | tf_op jit(solution)/shard_map/ppermute | solution.py:16
  182.6 1.2 fusion.32
  183.7 2.7 reshape_squeeze.10
  186.4 2.9 copy.86
  189.3 2.5 reshape_squeeze.9
  191.9 40.3 %all-gather.9.cloned.1.call-done = bf16[5376,512]{1,0:T(8,128)(2,1)} async-done(((bf16[672,512]{1,0:T(8,128)(2,1)}), bf16[5376,512]{1,0:T(8,128)(2,1)}) %all-gather.9.cloned.1.call-update) | async-done | bytes 5505040 | tf_op jit(solution)/shard_map/all_gather | solution.py:121
  232.2 5.0 %fusion.35 = f32[256,512]{1,0:T(8,128)} fusion(bf16[256,5376]{1,0:T(8,128)(2,1)S(1)} %copy-done, bf16[5376,512]{1,0:T(8,128)(2,1)} %all-gather.9.cloned.1.call-done), kind=kOutput, calls=%fused_computation.92 | convolution fusion | flops 1409286144 | bytes 8781824 | tf_op jit(solution)/shard_map/dot_general | solution.py:126
  237.1 1.2 reshape.211
  241.1 1.4 multiply_multiply_fusion
  242.5 1.5 subtract_convert_fusion
  244.2 2.8 fusion.34
  247.1 2.3 select_reduce_fusion
  249.4 2.6 multiply_reduce_fusion.1
  252.1 3.1 fusion.1
  255.1 1.5 copy-done.3
  258.0 2.0 copy.102
  260.0 1.9 copy.103
  261.9 1.6 multiply_add_fusion.1
  264.5 1.3 multiply_reduce_fusion
  266.8 3.1 fusion.3
  269.9 4.7 %fusion.28 = f32[2,128,1280,1]{2,1,3,0:T(8,128)S(1)} fusion(bf16[256,2,2,128]{0,3,2,1:T(8,128)(2,1)S(1)} %bitcast.85, f32[2,2,256,1280]{2,3,1,0:T(8,128)} %copy-done.4, f32[2,2,256]{2,1,0:T(2,128)S(1)} %copy-done.33, s32[2,2]{1,0:T(2,128)S(1)} %copy-done.37, s32[256,1280]{0,1:T(8,128)S(1)} %copy-done.6, pred[1280]{0:T(1024)(128)(4,1)S(1)} %copy-done.28, ...), kind=kOutput, calls=%fused_computation.87 | convolution fusion | flops 343408640 | bytes 8459536 | tf_op jit(solution)/shard_map/gjts,tgjd->sgd/dot_general | solution.py:79
  274.8 1.2 fusion.31
  276.0 3.4 collective-permute-start.4
  279.4 2.1 collective-permute-start.5
  281.5 4.2 collective-permute-start.6
  285.7 2.0 collective-permute-start.7
  288.3 1.5 copy.74
  289.8 2.2 fusion.8
  294.0 2.7 collective-permute-done.5
  296.6 5.7 %collective-permute-done.6 = bf16[2,256,256]{1,2,0:T(8,128)(2,1)} collective-permute-done((bf16[2,256,256]{1,2,0:T(8,128)(2,1)}, bf16[2,256,256]{1,2,0:T(8,128)(2,1)}, u32[]{:S(2)}, u32[]{:S(2)}) %collective-permute-start.6) | collective-permute-done | bytes 262176 | tf_op jit(solution)/shard_map/ppermute | solution.py:16
  302.4 27.3 %collective-permute-done.7 = bf16[2,256,256]{1,2,0:T(8,128)(2,1)} collective-permute-done((bf16[2,256,256]{1,2,0:T(8,128)(2,1)}, bf16[2,256,256]{1,2,0:T(8,128)(2,1)}, u32[]{:S(2)}, u32[]{:S(2)}) %collective-permute-start.7) | collective-permute-done | bytes 262176 | tf_op jit(solution)/shard_map/ppermute | solution.py:16
  329.6 1.3 fusion.13
  333.1 69.3 %all-gather.11.cloned.1.call-done = bf16[5376,1024]{1,0:T(8,128)(2,1)} async-done(((bf16[672,1024]{1,0:T(8,128)(2,1)}), bf16[5376,1024]{1,0:T(8,128)(2,1)}) %all-gather.11.cloned.1.call-update) | async-done | bytes 11010064 | tf_op jit(solution)/shard_map/all_gather | solution.py:173
  402.4 8.9 %convolution_convert_fusion = bf16[256,5376]{0,1:T(8,128)(2,1)} fusion(bf16[5376,1024]{1,0:T(8,128)(2,1)} %all-gather.11.cloned.1.call-done, bf16[256,256]{1,0:T(8,128)(2,1)S(1)} %copy.79, bf16[256,256]{1,0:T(8,128)(2,1)S(1)} %copy.78, bf16[256,512]{1,0:T(8,128)(2,1)} %bitcast.86), kind=kOutput, calls=%fused_computation | convolution fusion | flops 2821521408 | bytes 14286848 | tf_op jit(solution)/shard_map/dot_general | solution.py:171
  413.1 45.4 %reduce-scatter.2.cloned.1.call-done = bf16[256,1344]{0,1:T(8,128)(2,1)} async-done(((bf16[256,5376]{0,1:T(8,128)(2,1)}), bf16[256,1344]{0,1:T(8,128)(2,1)}) %reduce-scatter.2.cloned.1.call-update) | async-done | bytes 688144 | tf_op jit(solution)/shard_map/reduce_scatter | solution.py:177
  (135 shorter events, 23.6 us)
Async XLA Ops:
  7.2 58.9 %copy-start = (bf16[256,5376]{1,0:T(8,128)(2,1)S(1)}, bf16[256,5376]{1,0:T(8,128)(2,1)}, u32[]{:S(2)}) copy-start(bf16[256,5376]{1,0:T(8,128)(2,1)} %param.10) | copy-start | bytes 8257540
  7.2 58.9 %all-gather.5.cloned.1.call-start = ((), (), s32[]{:S(2)}) async-start(), calls=%async_computation.1 | async-start | bytes 3096576 | tf_op jit(solution)/shard_map/all_gather | solution.py:122
  7.9 4.3 copy-start.34
  7.9 4.3 copy-start.35
  7.9 115.0 %all-gather.7.cloned.1.call-start = ((), (), s32[]{:S(2)}) async-start(), calls=%async_computation.2 | async-start | bytes 3096576 | tf_op jit(solution)/shard_map/all_gather | solution.py:123
  8.7 223.5 %all-gather.9.cloned.1.call-start = ((), (), s32[]{:S(2)}) async-start(), calls=%async_computation.3 | async-start | bytes 6193152 | tf_op jit(solution)/shard_map/all_gather | solution.py:121
  9.4 393.0 %all-gather.11.cloned.1.call-start = ((), (), s32[]{:S(2)}) async-start(), calls=%async_computation.4 | async-start | bytes 12386304 | tf_op jit(solution)/shard_map/all_gather | solution.py:173
  12.1 446.5 %reduce-scatter.2.cloned.1.call-start = ((), (), s32[]{:S(2)}) async-start(), calls=%async_computation.5 | async-start | bytes 3440640 | tf_op jit(solution)/shard_map/reduce_scatter | solution.py:177
  29.2 39.9 %copy-start.12 = (f32[256,64]{1,0:T(8,128)}, f32[256,64]{1,0:T(8,128)S(1)}, u32[]{:S(2)}) copy-start(f32[256,64]{1,0:T(8,128)S(1)} %get-tuple-element.24) | copy-start | bytes 196612
  29.2 39.9 %copy-start.13 = (f32[256,64]{1,0:T(8,128)}, f32[256,64]{1,0:T(8,128)S(1)}, u32[]{:S(2)}) copy-start(f32[256,64]{1,0:T(8,128)S(1)} %get-tuple-element.25) | copy-start | bytes 196612
  29.3 39.9 %copy-start.19 = (f32[256,64]{0,1:T(8,128)}, f32[256,64]{0,1:T(8,128)S(1)}, u32[]{:S(2)}) copy-start(f32[256,64]{0,1:T(8,128)S(1)} %copy.56) | copy-start | bytes 196612
  29.4 39.9 %copy-start.21 = (f32[256,64]{0,1:T(8,128)}, f32[256,64]{0,1:T(8,128)S(1)}, u32[]{:S(2)}) copy-start(f32[256,64]{0,1:T(8,128)S(1)} %copy.57) | copy-start | bytes 196612
  32.5 36.6 %copy-start.30 = (f32[128]{0:T(128)S(1)}, f32[128]{0:T(128)}, u32[]{:S(2)}) copy-start(f32[128]{0:T(128)} %param.15) | copy-start | bytes 1540
  69.4 62.8 %copy-start.38 = (s32[4]{0:T(128)S(1)}, s32[4]{0:T(128)}, u32[]{:S(2)}) copy-start(s32[4]{0:T(128)} %param.16) | copy-start | bytes 52
  123.0 6.0 %copy-start.23 = (bf16[256,512]{1,0:T(8,128)(2,1)S(1)}, bf16[256,512]{1,0:T(8,128)(2,1)}, u32[]{:S(2)}) copy-start(bf16[256,512]{1,0:T(8,128)(2,1)} %param.19) | copy-start | bytes 786436
  126.4 15.4 %collective-permute-start = (bf16[2,256,256]{2,1,0:T(8,128)(2,1)}, bf16[2,256,256]{2,1,0:T(8,128)(2,1)}, u32[]{:S(2)}, u32[]{:S(2)}) collective-permute-start(bf16[2,256,256]{2,1,0:T(8,128)(2,1)} %pad_maximum_fusion.2), channel_id=1, source_target_pairs={{0,16},{4,20},{8,24},{12,28},{1,17},{5,21},{9,25},{13,29},{2,18},{... | collective-permute-start | bytes 786440 | tf_op jit(solution)/shard_map/ppermute | solution.py:16
  127.7 43.5 %collective-permute-start.1 = (bf16[2,256,256]{2,1,0:T(8,128)(2,1)}, bf16[2,256,256]{2,1,0:T(8,128)(2,1)}, u32[]{:S(2)}, u32[]{:S(2)}) collective-permute-start(bf16[2,256,256]{2,1,0:T(8,128)(2,1)} %pad_maximum_fusion.2), channel_id=1, source_target_pairs={{0,12},{4,16},{8,20},{12,24},{16,28},{1,13},{5,17},{9,21},{13,25},... | collective-permute-start | bytes 786440 | tf_op jit(solution)/shard_map/ppermute | solution.py:16
  129.1 52.4 %collective-permute-start.2 = (bf16[2,256,256]{2,1,0:T(8,128)(2,1)}, bf16[2,256,256]{2,1,0:T(8,128)(2,1)}, u32[]{:S(2)}, u32[]{:S(2)}) collective-permute-start(bf16[2,256,256]{2,1,0:T(8,128)(2,1)} %pad_maximum_fusion.2), channel_id=1, source_target_pairs={{0,8},{4,12},{8,16},{12,20},{16,24},{20,28},{1,9},{5,13},{9,17},{1... | collective-permute-start | bytes 786440 | tf_op jit(solution)/shard_map/ppermute | solution.py:16
  133.7 48.8 %collective-permute-start.3 = (bf16[2,256,256]{2,1,0:T(8,128)(2,1)}, bf16[2,256,256]{2,1,0:T(8,128)(2,1)S(1)}, u32[]{:S(2)}, u32[]{:S(2)}) collective-permute-start(bf16[2,256,256]{2,1,0:T(8,128)(2,1)} %pad_maximum_fusion.2), channel_id=1, source_target_pairs={{0,4},{4,8},{8,12},{12,16},{16,20},{20,24},{24,28},{1,5},{5,9},{9,... | collective-permute-start | bytes 786440 | tf_op jit(solution)/shard_map/ppermute | solution.py:16
  241.1 3.1 copy-start.5
  241.1 3.1 copy-start.11
  241.1 3.1 copy-start.14
  244.1 2.9 copy-start.16
  244.2 2.9 copy-start.17
  244.2 2.8 copy-start.27
  244.2 2.8 copy-start.36
  247.0 5.0 %copy-start.4 = (f32[2,2,256,1280]{2,3,1,0:T(8,128)}, f32[2,2,256,1280]{2,3,1,0:T(8,128)S(1)}, u32[]{:S(2)}) copy-start(f32[2,2,256,1280]{2,3,1,0:T(8,128)S(1)} %get-tuple-element.29) | copy-start | bytes 15728644
  247.1 2.3 copy-start.18
  247.1 2.3 copy-start.25
  249.4 2.7 copy-start.32
  255.1 1.5 copy-start.3
  257.1 7.3 %copy-start.29 = (f32[128]{0:T(128)S(1)}, f32[128]{0:T(128)}, u32[]{:S(2)}) copy-start(f32[128]{0:T(128)} %param.14) | copy-start | bytes 1540
  266.7 3.1 copy-start.6
  266.7 3.1 copy-start.15
  266.7 3.1 copy-start.26
  266.7 3.1 copy-start.28
  266.8 3.1 copy-start.33
  266.8 3.1 copy-start.37
  269.9 4.7 %copy-start.1 = (f32[2,128,1280]{2,1,0:T(8,128)}, f32[2,128,1280]{2,1,0:T(8,128)S(1)}, u32[]{:S(2)}) copy-start(f32[2,128,1280]{2,1,0:T(8,128)S(1)} %fusion.3) | copy-start | bytes 3932164
  276.0 18.0 %collective-permute-start.4 = (bf16[2,256,256]{1,2,0:T(8,128)(2,1)}, bf16[2,256,256]{1,2,0:T(8,128)(2,1)}, u32[]{:S(2)}, u32[]{:S(2)}) collective-permute-start(bf16[2,256,256]{1,2,0:T(8,128)(2,1)} %get-tuple-element.10), channel_id=1, source_target_pairs={{4,0},{8,4},{12,8},{16,12},{20,16},{24,20},{28,24},{5,1},{9,5},{13... | collective-permute-start | bytes 786440 | tf_op jit(solution)/shard_map/ppermute | solution.py:16
  279.4 17.2 %collective-permute-start.5 = (bf16[2,256,256]{1,2,0:T(8,128)(2,1)}, bf16[2,256,256]{1,2,0:T(8,128)(2,1)}, u32[]{:S(2)}, u32[]{:S(2)}) collective-permute-start(bf16[2,256,256]{1,2,0:T(8,128)(2,1)} %get-tuple-element.13), channel_id=1, source_target_pairs={{8,0},{12,4},{16,8},{20,12},{24,16},{28,20},{9,1},{13,5},{17,9},{2... | collective-permute-start | bytes 786440 | tf_op jit(solution)/shard_map/ppermute | solution.py:16
  281.5 20.9 %collective-permute-start.6 = (bf16[2,256,256]{1,2,0:T(8,128)(2,1)}, bf16[2,256,256]{1,2,0:T(8,128)(2,1)}, u32[]{:S(2)}, u32[]{:S(2)}) collective-permute-start(bf16[2,256,256]{1,2,0:T(8,128)(2,1)} %get-tuple-element.12), channel_id=1, source_target_pairs={{12,0},{16,4},{20,8},{24,12},{28,16},{13,1},{17,5},{21,9},{25,13},... | collective-permute-start | bytes 786440 | tf_op jit(solution)/shard_map/ppermute | solution.py:16
  285.7 44.0 %collective-permute-start.7 = (bf16[2,256,256]{1,2,0:T(8,128)(2,1)}, bf16[2,256,256]{1,2,0:T(8,128)(2,1)}, u32[]{:S(2)}, u32[]{:S(2)}) collective-permute-start(bf16[2,256,256]{1,2,0:T(8,128)(2,1)} %get-tuple-element.11), channel_id=1, source_target_pairs={{16,0},{20,4},{24,8},{28,12},{17,1},{21,5},{25,9},{29,13},{18,2},{... | collective-permute-start | bytes 786440 | tf_op jit(solution)/shard_map/ppermute | solution.py:16
  289.8 39.9 %copy-start.2 = (f32[2,128,1280]{2,1,0:T(8,128)S(1)}, f32[2,128,1280]{2,1,0:T(8,128)}, u32[]{:S(2)}) copy-start(f32[2,128,1280]{2,1,0:T(8,128)} %copy-done.1) | copy-start | bytes 3932164
  289.8 39.9 %copy-start.8 = (f32[2,128,1280,1]{2,1,3,0:T(8,128)S(1)}, f32[2,128,1280,1]{2,1,3,0:T(8,128)}, u32[]{:S(2)}) copy-start(f32[2,128,1280,1]{2,1,3,0:T(8,128)} %copy-done.7) | copy-start | bytes 3932164
  292.0 39.0 %copy-start.20 = (f32[256,64]{0,1:T(8,128)S(1)}, f32[256,64]{0,1:T(8,128)}, u32[]{:S(2)}) copy-start(f32[256,64]{0,1:T(8,128)} %copy-done.19) | copy-start | bytes 196612
  292.1 39.0 %copy-start.22 = (f32[256,64]{0,1:T(8,128)S(1)}, f32[256,64]{0,1:T(8,128)}, u32[]{:S(2)}) copy-start(f32[256,64]{0,1:T(8,128)} %copy-done.21) | copy-start | bytes 196612
  292.8 38.3 %copy-start.31 = (f32[128]{0:T(128)S(1)}, f32[128]{0:T(128)}, u32[]{:S(2)}) copy-start(f32[128]{0:T(128)} %param.15) | copy-start | bytes 1540
  (4 other events, 4.1 us)
Sparse Core Ops, SparseCore 0:
  10.2 55.8 all-gather.4
  68.3 54.6 all-gather.6
  125.1 106.9 all-gather.8
  234.2 168.1 all-gather.10
  411.5 47.0 reduce-scatter.1
where the time goes:
time: 468 us; the launch traced here: 465 us
  waiting for transfers between devices  325 us (69%)
  matrix products  36.2 us (8%)
  local copies, waits for them, and re-layouts  31.6 us (7%)
  other arithmetic  22.2 us (5%)
  starting transfers between devices  19.3 us (4%)
  blocking collectives  15.8 us (3%)
  between operations  15.2 us (3%)
    ppermute x8, waiting for transfers between devices, passed_along(): return lax.ppermute(block, axis, route)  80.4 us
    all_gather x1, waiting for transfers between devices, body(): lax.all_gather(joined_rows, 'seq', axis=0, tiled=True)  69.3 us
    all_gather x1, waiting for transfers between devices, body(): lax.all_gather(row_pieces[2], 'seq', axis=0, tiled=True)  53.6 us
    reduce_scatter x1, waiting for transfers between devices, body(): lax.psum_scatter(partial_grad.astype(jnp.bfloat16), 'head', scatter_dimen...  45.4 us
    all_gather x1, waiting for transfers between devices, body(): lax.all_gather(row_pieces[0], 'seq', axis=0, tiled=True)  40.3 us
    all_gather x1, waiting for transfers between devices, body(): lax.all_gather(row_pieces[1], 'seq', axis=0, tiled=True)  33.6 us
    ppermute x8, starting transfers between devices, passed_along(): return lax.ppermute(block, axis, route)  19.1 us
    psum x1, blocking collectives, body(): normalizer = lax.psum(jnp.sum(kept_weight), 'seq')  15.8 us
  transfers between devices with their start and end apart: 13, of which 12 were waited for; matrix products, arithmetic and copies ran while one was open for 17% of the time, Pallas kernels for 0%

commit v1 on v0

v1 whole, which is shorter than its diff:
```python
import functools

import jax
import jax.numpy as jnp
from jax import lax
from jax.experimental import pallas as pl
from jax.experimental.pallas import tpu as pltpu
from jax.sharding import PartitionSpec as P

QPRE = 168
WINDOW = 1024
NORM_EPS = 1e-06
MESH = pl.DeviceIdType.MESH


def ring_place(index, n):
    return jnp.where(index % 2 == 0, index // 2, n - 1 - index // 2)


def ring_index(place, n):
    return jnp.where(place < n // 2, 2 * place, 2 * (n - 1 - place) + 1)


def row_cuts(rows, parts):
    if rows % 16 or rows < 16 * parts:
        return [(0, rows)]
    units = rows // 16
    edges = [16 * (units * i // parts) for i in range(parts + 1)]
    return [(a, b - a) for a, b in zip(edges, edges[1:])]


def ring_gather(n, jobs, me, send_sems, recv_sems, middle=None):
    place = ring_place(me, n)

    def at(distance):
        return ring_index(lax.rem(place + distance + n, n), n)

    def copy(step, job):
        source, dest, way = jobs[job]
        owner = at(-way * step)
        return pltpu.make_async_remote_copy(
            src_ref=dest(owner),
            dst_ref=dest(owner),
            send_sem=send_sems.at[step, job],
            recv_sem=recv_sems.at[step, job],
            device_id={"seq": at(way)},
            device_id_type=MESH,
        )

    def first(job):
        source, dest, way = jobs[job]
        return pltpu.make_async_remote_copy(
            src_ref=source,
            dst_ref=dest(me),
            send_sem=send_sems.at[0, job],
            recv_sem=recv_sems.at[0, job],
            device_id={"seq": at(way)},
            device_id_type=MESH,
        )

    for job in range(len(jobs)):
        first(job).start()
    if middle is not None:
        middle()

    def arrived(step, job):
        source, dest, way = jobs[job]
        owner = at(-way * (step + 1))
        return pltpu.make_async_remote_copy(
            src_ref=dest(owner),
            dst_ref=dest(owner),
            send_sem=send_sems.at[step, job],
            recv_sem=recv_sems.at[step, job],
            device_id={"seq": at(way)},
            device_id_type=MESH,
        )

    def body(step, carry):
        for job in range(len(jobs)):
            arrived(step - 1, job).wait_recv()
            copy(step, job).start()
        return carry

    lax.fori_loop(1, n - 1, body, 0)
    for job in range(len(jobs)):
        arrived(n - 2, job).wait_recv()

    def drain(step, carry):
        for job in range(len(jobs)):
            arrived(step, job).wait_send()
        return carry

    lax.fori_loop(0, n - 1, drain, 0)


def greet(peers):
    barrier = pltpu.get_barrier_semaphore()
    for peer in peers:
        pl.semaphore_signal(barrier, inc=1, device_id={"seq": peer}, device_id_type=MESH)
    pl.semaphore_wait(barrier, len(peers))


def greet_near(n, me, reach):
    barrier = pltpu.get_barrier_semaphore()
    for step in range(1, reach + 1):
        for peer, there in ((me + step, me + step < n), (me - step, me >= step)):

            @pl.when(there)
            def _():
                pl.semaphore_signal(barrier, inc=1, device_id={"seq": peer}, device_id_type=MESH)

    pl.semaphore_wait(barrier, jnp.minimum(me, reach) + jnp.minimum(n - 1 - me, reach))


def kv_gather_kernel(n, k_ref, v_ref, tile_ref, kv_out, tile_out, send, recv, local):
    me = lax.axis_index("seq")
    rows, width = k_ref.shape
    place = ring_place(me, n)
    greet([ring_index(lax.rem(place + d + n, n), n) for d in (1, -1)])
    own = [
        pltpu.make_async_copy(k_ref, kv_out.at[me, :, pl.ds(0, width)], local.at[0]),
        pltpu.make_async_copy(v_ref, kv_out.at[me, :, pl.ds(width, width)], local.at[1]),
        pltpu.make_async_copy(tile_ref, tile_out.at[me], local.at[2]),
    ]
    jobs = []
    for a, size in row_cuts(rows, 2):
        jobs.append(
            (
                k_ref.at[pl.ds(a, size)],
                lambda owner, a=a, size=size: kv_out.at[owner, pl.ds(a, size), pl.ds(0, width)],
                1,
            )
        )
        jobs.append(
            (
                v_ref.at[pl.ds(a, size)],
                lambda owner, a=a, size=size: kv_out.at[owner, pl.ds(a, size), pl.ds(width, width)],
                -1,
            )
        )
    jobs.append((tile_ref, lambda owner: tile_out.at[owner], 1))

    def middle():
        for c in own:
            c.start()

    ring_gather(n, jobs, me, send, recv, middle)
    for c in own:
        c.wait()


def kv_gather(n, k_weight, v_weight, tile):
    rows, width = k_weight.shape
    jobs = 2 * len(row_cuts(rows, 2)) + 1
    hbm = pl.BlockSpec(memory_space=pl.ANY)
    return pl.pallas_call(
        functools.partial(kv_gather_kernel, n),
        out_shape=[
            jax.ShapeDtypeStruct((n, rows, 2 * width), jnp.bfloat16),
            jax.ShapeDtypeStruct((n,) + tile.shape, jnp.float32),
        ],
        in_specs=[hbm] * 3,
        out_specs=[hbm] * 2,
        scratch_shapes=[
            pltpu.SemaphoreType.DMA((n - 1, jobs)),
            pltpu.SemaphoreType.DMA((n - 1, jobs)),
            pltpu.SemaphoreType.DMA((3,)),
        ],
        compiler_params=pltpu.CompilerParams(collective_id=0, has_side_effects=True),
    )(k_weight, v_weight, tile)


def near_copies(n, me, reach, way, source, dest, send, recv):
    result = []
    for step in range(reach, 0, -1):
        peer = me + way * step
        goes = peer < n if way > 0 else peer >= 0
        back = me - way * step
        comes = back >= 0 if way > 0 else back < n
        copy = pltpu.make_async_remote_copy(
            src_ref=source(step),
            dst_ref=dest(step),
            send_sem=send.at[step - 1],
            recv_sem=recv.at[step - 1],
            device_id={"seq": peer},
            device_id_type=MESH,
        )
        result.append((copy, goes, comes))
    return result


def start_near(copies):
    for copy, goes, _ in copies:
        pl.when(goes)(copy.start)


def finish_near(copies):
    for copy, goes, comes in copies:
        pl.when(goes)(copy.wait_send)
        pl.when(comes)(copy.wait_recv)


def q_gather_kernel(n, reach, q_ref, kv_ref, q_out, near_out, send, recv, nsend, nrecv, local):
    me = lax.axis_index("seq")
    rows = q_ref.shape[0]
    greet_near(n, me, reach)
    own = pltpu.make_async_copy(q_ref, q_out.at[me], local.at[0])
    copies = near_copies(
        n, me, reach, 1, lambda step: kv_ref, lambda step: near_out.at[step - 1], nsend, nrecv
    )
    cuts = row_cuts(rows, 4)
    jobs = []
    for i, (a, size) in enumerate(cuts):
        jobs.append(
            (
                q_ref.at[pl.ds(a, size)],
                lambda owner, a=a, size=size: q_out.at[owner, pl.ds(a, size)],
                1 if i % 2 == 0 else -1,
            )
        )

    start_near(copies)
    ring_gather(n, jobs, me, send, recv, own.start)
    own.wait()
    finish_near(copies)


def q_gather(n, reach, q_weight, kv_own):
    rows, width = q_weight.shape
    jobs = len(row_cuts(rows, 4))
    hbm = pl.BlockSpec(memory_space=pl.ANY)
    return pl.pallas_call(
        functools.partial(q_gather_kernel, n, reach),
        out_shape=[
            jax.ShapeDtypeStruct((n, rows, width), jnp.bfloat16),
            jax.ShapeDtypeStruct((reach,) + kv_own.shape, jnp.bfloat16),
        ],
        in_specs=[hbm] * 2,
        out_specs=[hbm] * 2,
        scratch_shapes=[
            pltpu.SemaphoreType.DMA((n - 1, jobs)),
            pltpu.SemaphoreType.DMA((n - 1, jobs)),
            pltpu.SemaphoreType.DMA((reach,)),
            pltpu.SemaphoreType.DMA((reach,)),
            pltpu.SemaphoreType.DMA((1,)),
        ],
        compiler_params=pltpu.CompilerParams(collective_id=1, has_side_effects=True),
    )(q_weight, kv_own)


def give_back_kernel(n, reach, near_ref, near_out, send, recv):
    me = lax.axis_index("seq")
    greet_near(n, me, reach)
    copies = near_copies(
        n,
        me,
        reach,
        -1,
        lambda step: near_ref.at[step - 1],
        lambda step: near_out.at[step - 1],
        send,
        recv,
    )
    start_near(copies)
    finish_near(copies)


def give_back(n, reach, near):
    hbm = pl.BlockSpec(memory_space=pl.ANY)
    return pl.pallas_call(
        functools.partial(give_back_kernel, n, reach),
        out_shape=jax.ShapeDtypeStruct(near.shape, jnp.bfloat16),
        in_specs=[hbm],
        out_specs=hbm,
        scratch_shapes=[
            pltpu.SemaphoreType.DMA((reach,)),
            pltpu.SemaphoreType.DMA((reach,)),
        ],
        compiler_params=pltpu.CompilerParams(collective_id=2, has_side_effects=True),
    )(near)


def swap_halves(x):
    half = x.shape[-1] // 2
    return jnp.concatenate([x[:, half:], x[:, :half]], axis=1)


def rotate(u, gain, cosine, sine):
    mean_square = jnp.mean(u * u, axis=-1, keepdims=True)
    m = u * lax.rsqrt(mean_square + NORM_EPS) * gain
    return m * cosine + swap_halves(m) * sine


def rotate_back(u, gain, cosine, sine, grad):
    r = lax.rsqrt(jnp.mean(u * u, axis=-1, keepdims=True) + NORM_EPS)
    dn = (grad * cosine + swap_halves(grad * sine)) * gain
    return r * dn - u * (r * r * r) * jnp.mean(u * dn, axis=-1, keepdims=True)


def kv_ready_kernel(lin_ref, gain_ref, cos_ref, sin_ref, out_ref):
    width = gain_ref.shape[1]
    half = lin_ref.shape[1] // 2
    for g in range(half // width):
        cols = slice(g * width, (g + 1) * width)
        out_ref[:, cols] = rotate(
            lin_ref[:, cols], gain_ref[...], cos_ref[...], sin_ref[...]
        ).astype(jnp.bfloat16)
    out_ref[:, half:] = lin_ref[:, half:].astype(jnp.bfloat16)


def kv_back_kernel(reach, own_ref, near_ref, there_ref, lin_ref, gain_ref, cos_ref, sin_ref, out_ref):
    width = gain_ref.shape[1]
    full = lin_ref.shape[1]
    half = full // 2
    for g in range(full // width):
        cols = slice(g * width, (g + 1) * width)
        total = own_ref[:, cols]
        for step in range(reach):
            part = near_ref[step, :, cols].astype(jnp.float32)
            total = total + jnp.where(there_ref[step] > 0, part, 0.0)
        if g * width < half:
            total = rotate_back(
                lin_ref[:, cols], gain_ref[...], cos_ref[...], sin_ref[...], total
            )
        out_ref[:, cols] = total.astype(jnp.bfloat16)


def attend_kernel(
    reach,
    kv_heads,
    scale,
    there_ref,
    windows_ref,
    lin_ref,
    own_ref,
    near_ref,
    grad_ref,
    factor_ref,
    gain_ref,
    cos_ref,
    sin_ref,
    attn_ref,
    dq_ref,
    down_ref,
    dnear_ref,
    keys,
    soft,
    acc,
):
    rows = own_ref.shape[0]
    width = gain_ref.shape[1]
    q_heads = lin_ref.shape[1] // width
    group = q_heads // kv_heads
    keys[0] = own_ref[...]
    for step in range(1, reach + 1):
        keys[step] = jnp.where(there_ref[step - 1] > 0, near_ref[step - 1], 0)
    acc[...] = jnp.zeros_like(acc)
    gap = lax.broadcasted_iota(jnp.int32, (rows, rows), 0) - lax.broadcasted_iota(
        jnp.int32, (rows, rows), 1
    )
    last = (((1,), (1,)), ((), ()))
    first = (((0,), (0,)), ((), ()))

    def head(h, carry):
        cols = pl.ds(pl.multiple_of(h * width, width), width)
        kcols = pl.ds(pl.multiple_of(h // group * width, width), width)
        vcols = pl.ds(pl.multiple_of((kv_heads + h // group) * width, width), width)
        u = lin_ref[:, cols]
        q = rotate(u, gain_ref[...], cos_ref[...], sin_ref[...]).astype(jnp.bfloat16)
        cot = (grad_ref[:, cols].astype(jnp.float32) * factor_ref[...]).astype(jnp.bfloat16)
        peak = jnp.full((rows, 1), -1e30, jnp.float32)
        for b in range(reach + 1):
            s = scale * lax.dot_general(
                q, keys[b, :, kcols], last, preferred_element_type=jnp.float32
            )
            distance = gap + b * rows
            limit = windows_ref[h]
            if b == 0:
                ok = (distance >= 0) & (distance < limit)
            else:
                ok = distance < jnp.where(there_ref[b - 1] > 0, limit, 0)
            s = jnp.where(ok, s, -1e30)
            soft[b] = s
            peak = jnp.maximum(peak, jnp.max(s, axis=-1, keepdims=True))
        total = jnp.zeros((rows, 1), jnp.float32)
        for b in range(reach + 1):
            e = jnp.exp(soft[b] - peak)
            soft[b] = e
            total = total + jnp.sum(e, axis=-1, keepdims=True)
        inverse = 1.0 / total
        out = jnp.zeros((rows, width), jnp.float32)
        for b in range(reach + 1):
            p = soft[b] * inverse
            soft[b] = p
            pb = p.astype(jnp.bfloat16)
            out = out + jnp.dot(pb, keys[b, :, vcols], preferred_element_type=jnp.float32)
            acc[b, :, vcols] += lax.dot_general(
                pb, cot, first, preferred_element_type=jnp.float32
            )
        out = out.astype(jnp.bfloat16)
        attn_ref[:, cols] = out
        delta = jnp.sum(
            cot.astype(jnp.float32) * out.astype(jnp.float32), axis=-1, keepdims=True
        )
        dq = jnp.zeros((rows, width), jnp.float32)
        for b in range(reach + 1):
            dp = lax.dot_general(
                cot, keys[b, :, vcols], last, preferred_element_type=jnp.float32
            )
            ds = (soft[b] * (dp - delta)).astype(jnp.bfloat16)
            dq = dq + jnp.dot(ds, keys[b, :, kcols], preferred_element_type=jnp.float32)
            acc[b, :, kcols] += scale * lax.dot_general(
                ds, q, first, preferred_element_type=jnp.float32
            )
        dq_ref[:, cols] = rotate_back(
            u, gain_ref[...], cos_ref[...], sin_ref[...], scale * dq
        ).astype(jnp.bfloat16)
        return carry

    lax.fori_loop(0, q_heads, head, 0)
    down_ref[...] = acc[0]
    for step in range(1, reach + 1):
        dnear_ref[step - 1] = acc[step].astype(jnp.bfloat16)


VMEM = pl.BlockSpec(memory_space=pltpu.VMEM)
SMEM = pl.BlockSpec(memory_space=pltpu.SMEM)
ROOM = pltpu.CompilerParams(vmem_limit_bytes=40 * 1024 * 1024)


def body(
    tokens,
    q_weight,
    k_weight,
    v_weight,
    q_gain,
    k_gain,
    windows,
    token_weight,
    loss_mask,
    grad_attn,
):
    n = lax.axis_size("seq")
    me = lax.axis_index("seq")
    tok_rows, depth = tokens.shape
    head_width = q_gain.shape[0]
    q_cols = q_weight.shape[1]
    kv_cols = 2 * k_weight.shape[1]
    kv_heads = k_weight.shape[1] // head_width
    reach = WINDOW // tok_rows
    scale = QPRE ** (-0.5)
    f32 = jnp.float32

    kept = token_weight * loss_mask.astype(f32)
    tile = jnp.broadcast_to(jnp.sum(kept), (8, 128))
    kv_full, tiles = kv_gather(n, k_weight, v_weight, tile)
    normalizer = jnp.sum(tiles[:, 0, 0])
    factor = (kept * (tok_rows * n / normalizer))[:, None]

    positions = me * tok_rows + jnp.arange(tok_rows, dtype=jnp.int32)
    half_width = head_width // 2
    frequency = 10000.0 ** (-(jnp.arange(half_width, dtype=f32) * 2.0) / head_width)
    angles = positions.astype(f32)[:, None] * frequency[None, :]
    cosine, sine = jnp.cos(angles), jnp.sin(angles)
    cosine = jnp.concatenate([cosine, cosine], axis=1)
    sine = jnp.concatenate([-sine, sine], axis=1)
    steps = jnp.arange(1, reach + 1, dtype=jnp.int32)
    before = (me >= steps).astype(jnp.int32)
    after = (me + steps < n).astype(jnp.int32)
    q_gain = q_gain[None, :]
    k_gain = k_gain[None, :]

    kv_matrix = kv_full.reshape(depth, kv_cols)
    kv_lin = jnp.dot(tokens, kv_matrix, preferred_element_type=f32)
    kv_own = pl.pallas_call(
        kv_ready_kernel,
        out_shape=jax.ShapeDtypeStruct((tok_rows, kv_cols), jnp.bfloat16),
        in_specs=[VMEM] * 4,
        out_specs=VMEM,
        compiler_params=ROOM,
    )(kv_lin, k_gain, cosine, sine)
    q_full, near = q_gather(n, reach, q_weight, kv_own)
    q_matrix = q_full.reshape(depth, q_cols)
    q_lin = jnp.dot(tokens, q_matrix, preferred_element_type=f32)
    attended, dq_lin, down, dnear = pl.pallas_call(
        functools.partial(attend_kernel, reach, kv_heads, scale),
        out_shape=[
            jax.ShapeDtypeStruct((tok_rows, q_cols), jnp.bfloat16),
            jax.ShapeDtypeStruct((tok_rows, q_cols), jnp.bfloat16),
            jax.ShapeDtypeStruct((tok_rows, kv_cols), f32),
            jax.ShapeDtypeStruct((reach, tok_rows, kv_cols), jnp.bfloat16),
        ],
        in_specs=[SMEM] * 2 + [VMEM] * 8,
        out_specs=[VMEM] * 4,
        scratch_shapes=[
            pltpu.VMEM((reach + 1, tok_rows, kv_cols), jnp.bfloat16),
            pltpu.VMEM((reach + 1, tok_rows, tok_rows), f32),
            pltpu.VMEM((reach + 1, tok_rows, kv_cols), f32),
        ],
        compiler_params=ROOM,
    )(before, windows, q_lin, kv_own, near, grad_attn, factor, q_gain, cosine, sine)
    returned = give_back(n, reach, dnear)
    dkv_lin = pl.pallas_call(
        functools.partial(kv_back_kernel, reach),
        out_shape=jax.ShapeDtypeStruct((tok_rows, kv_cols), jnp.bfloat16),
        in_specs=[VMEM, VMEM, SMEM] + [VMEM] * 4,
        out_specs=VMEM,
        compiler_params=ROOM,
    )(down, returned, after, kv_lin, k_gain, cosine, sine)
    contract = (((1,), (1,)), ((), ()))
    partial_grad = lax.dot_general(
        dq_lin, q_matrix, contract, preferred_element_type=f32
    ) + lax.dot_general(dkv_lin, kv_matrix, contract, preferred_element_type=f32)
    grad_tokens = lax.psum_scatter(
        partial_grad.astype(jnp.bfloat16), "head", scatter_dimension=1, tiled=True
    )
    return (attended, grad_tokens)


def solution(mesh):
    in_specs = (
        P("seq", None),
        P("seq", "head"),
        P("seq", "head"),
        P("seq", "head"),
        P(),
        P(),
        P("head"),
        P("seq"),
        P("seq"),
        P("seq", "head"),
    )
    out_specs = (P("seq", "head"), P("seq", "head"))
    return jax.shard_map(body, mesh=mesh, in_specs=in_specs, out_specs=out_specs, check_vma=False)
```

time: 468 us -> 285 us (0.61)
  waiting for transfers between devices: 325 us -> 45.9 us
  Pallas kernels: 0 us -> 186 us
  matrix products: 36.2 us -> 16.7 us
  starting transfers between devices: 19.3 us -> 0.04 us
  local copies, waits for them, and re-layouts: 31.6 us -> 13.8 us
  other arithmetic: 22.2 us -> 5.94 us
  blocking collectives: 15.8 us -> 0 us
    all_gather x4 -> x0, waiting for transfers between devices: 197 us -> none  [the longest x1 69.3 us: body(): lax.all_gather(joined_rows, 'seq', axis=0, tiled=True)]
    pallas_call x0 -> x6, Pallas kernels: none -> 186 us  [the longest x1 91.3 us: q_gather(): pl.pallas_call(functools.partial(q_gather_kernel, n, reach), out_shape=[j...]
    ppermute x8 -> x0, waiting for transfers between devices: 80.4 us -> none  [passed_along(): return lax.ppermute(block, axis, route)]
    dot_general x10 -> x4, matrix products: 36.2 us -> 16.7 us  [the longest x1 4.97 us: body(): q_lin = jnp.dot(tokens, q_matrix, preferred_element_type=f32)]
    ppermute x8 -> x0, starting transfers between devices: 19.1 us -> none  [passed_along(): return lax.ppermute(block, axis, route)]
    psum x1 -> x0, blocking collectives: 15.8 us -> none  [body(): normalizer = lax.psum(jnp.sum(kept_weight), 'seq')]
    another operation x5 -> x0, local copies, waits for them, and re-layouts: 8.2 us -> none  [the longest x2 5.61 us: body(): key_rows = extended[0].reshape(key_span, kv_heads, head_width)]
    unnamed x86 -> x50, local copies, waits for them, and re-layouts: 12 us -> 11.1 us
  transfers between devices with their start and end apart: 13 -> 1, of which waited for: 12 -> 1; matrix products, arithmetic and copies ran while one was open for 17% -> 0% of each run, Pallas kernels for 0% -> 0%
where the time goes in v1:
time: 285 us; the launch traced here: 283 us
  Pallas kernels  186 us (65%)
  waiting for transfers between devices  45.9 us (16%)
  matrix products  16.7 us (6%)
  between operations  15 us (5%)
  local copies, waits for them, and re-layouts  13.8 us (5%)
  other arithmetic  5.94 us (2%)
    pallas_call x1, Pallas kernels, q_gather(): pl.pallas_call(functools.partial(q_gather_kernel, n, reach), out_shape=[j...  91.3 us
    pallas_call x1, Pallas kernels, kv_gather(): pl.pallas_call(functools.partial(kv_gather_kernel, n), out_shape=[jax.Sha...  55.8 us
    reduce_scatter x1, waiting for transfers between devices, body(): lax.psum_scatter(partial_grad.astype(jnp.bfloat16), 'head', scatter_dimen...  45.9 us
    pallas_call x1, Pallas kernels, give_back(): pl.pallas_call(functools.partial(give_back_kernel, n, reach), out_shape=j...  26.1 us
    pallas_call x1, Pallas kernels, body(): pl.pallas_call(functools.partial(attend_kernel, reach, kv_heads, scale),...  11.4 us
    unnamed x50, local copies, waits for them, and re-layouts  11.1 us
  transfers between devices with their start and end apart: 1, of which 1 were waited for; matrix products, arithmetic and copies ran while one was open for 0% of the time, Pallas kernels for 0%

profile of v1, /device:TPU:18, one launch (start us, length us, event | category | flops | bytes accessed | tf_op | source)
XLA Modules:
  0.0 283.3 jit_solution(8039289138590357586)
XLA Ops:
  7.2 0.0 copy-start
  7.2 0.0 reduce-scatter.2.cloned.1.call-start
  7.2 0.5 compare_convert_fusion
  7.8 1.2 fusion.1
  9.0 1.4 fusion.2
  10.3 1.3 broadcast_in_dim.14.tile_ref
  11.6 55.8 %shard_map.113 = (bf16[8,672,512]{2,1,0:T(8,128)(2,1)}, f32[8,8,128]{2,1,0:T(8,128)}) custom-call(bf16[672,256]{1,0:T(8,128)(2,1)} %k_ref.1, bf16[672,256]{1,0:T(8,128)(2,1)} %v_ref.1, f32[8,128]{1,0:T(8,128)} %broadcast_in_dim.14.tile_ref), custom_call_target="tpu_custom_call" | custom-call | tf_op jit(solution)/shard_map/pallas_call | solution.py:156
  67.4 0.0 copy-done
  67.4 0.0 copy-start.22
  67.4 0.0 copy-start.18
  67.4 4.2 %convolution_bitcast_fusion.1.lin_ref = f32[256,512]{1,0:T(8,128)S(1)} fusion(bf16[256,5376]{1,0:T(8,128)(2,1)S(1)} %copy-done, bf16[5376,512]{1,0:T(8,128)(2,1)} %bitcast.20), kind=kOutput, calls=%fused_computation.3 | convolution fusion | flops 1409286144 | bytes 8781824 | tf_op jit(solution)/shard_map/dot_general | solution.py:474
  71.6 0.1 pad_maximum_fusion
  71.8 0.0 copy-done.18
  71.8 0.3 shard_map.114.kv_ref.own_ref
  72.1 0.0 copy-start.2
  72.1 0.7 copy-done.2
  72.8 0.7 copy-done.4
  73.5 0.6 copy-done.7
  74.1 91.3 %shard_map.115 = (bf16[8,672,512]{2,1,0:T(8,128)(2,1)}, bf16[4,256,512]{2,1,0:T(8,128)(2,1)}) custom-call(bf16[672,512]{1,0:T(8,128)(2,1)} %q_ref.1, bf16[256,512]{1,0:T(8,128)(2,1)} %copy-done.2), custom_call_target="tpu_custom_call" | custom-call | tf_op jit(solution)/shard_map/pallas_call | solution.py:232
  165.4 0.0 copy-start.3
  165.4 0.0 copy-start.19
  165.4 0.0 copy-start.20
  165.4 5.0 %convolution_bitcast_fusion.lin_ref = f32[256,512]{1,0:T(8,128)} fusion(bf16[256,5376]{1,0:T(8,128)(2,1)S(1)} %copy-done, bf16[5376,512]{1,0:T(8,128)(2,1)} %bitcast.24), kind=kOutput, calls=%fused_computation.2 | convolution fusion | flops 1409286144 | bytes 8781824 | tf_op jit(solution)/shard_map/dot_general | solution.py:484
  170.4 1.5 slice_reduce_fusion
  172.6 1.2 broadcast_multiply_fusion
  173.8 1.4 copy.16.factor_ref
  175.2 0.9 copy-done.5
  176.1 0.9 copy-done.8
  177.0 1.2 copy-done.10
  178.3 1.0 copy-done.13
  179.3 0.9 copy-done.16
  180.2 0.9 copy-done.17
  181.2 0.6 copy-done.21
  181.8 11.4 %shard_map.116 = (bf16[256,512]{1,0:T(8,128)(2,1)}, bf16[256,512]{1,0:T(8,128)(2,1)S(1)}, f32[256,512]{1,0:T(8,128)S(1)}, bf16[4,256,512]{2,1,0:T(8,128)(2,1)S(1)}) custom-call(s32[4]{0:T(128)S(1)} %copy-done.21, s32[4]{0:T(128)S(1)} %copy-done.19, f32[256,512]{1,0:T(8,128)S(1)} %copy-done.13, bf16[256,512]{1,0:T(8,128)(2,1)S(1)} %copy-done.3, ...), custom_call_target="tpu_custom_call" | custom-call | tf_op jit(solution)/shard_map/pallas_call | solution.py:485
  193.2 1.0 copy-done.11
  194.2 0.7 copy-done.12
  194.9 0.8 copy-done.14
  195.7 26.1 %shard_map.117.near_ref = bf16[4,256,512]{2,1,0:T(8,128)(2,1)} custom-call(bf16[4,256,512]{2,1,0:T(8,128)(2,1)} %copy-done.11), custom_call_target="tpu_custom_call" | custom-call | tf_op jit(solution)/shard_map/pallas_call | solution.py:270
  221.8 0.0 slice-start
  221.8 0.0 copy-start.15
  221.8 0.0 slice-start.1
  221.8 4.4 %fusion.3 = f32[256,5376]{0,1:T(8,128)S(1)} fusion(bf16[256,512]{1,0:T(8,128)(2,1)} %copy-done.12, bf16[5376,512]{1,0:T(8,128)(2,1)} %bitcast.25), kind=kOutput, calls=%fused_computation.18 | convolution fusion | flops 1409286144 | bytes 11272192 | tf_op jit(solution)/shard_map/dot_general | solution.py:511
  226.3 1.0 shard_map.118
  227.3 0.0 slice-done
  227.3 0.0 slice-done.1
  227.3 3.2 %fusion = bf16[256,5376]{0,1:T(8,128)(2,1)} fusion(f32[256,5376]{0,1:T(8,128)S(1)} %fusion.3, bf16[256,512]{1,0:T(8,128)(2,1)S(1)} %shard_map.118, bf16[5376,512]{1,0:T(8,128)(2,1)S(1)} %bitcast.23), kind=kOutput, calls=%fused_computation.1 | convolution fusion | flops 1412038656 | bytes 14024704 | tf_op jit(solution)/shard_map/dot_general | solution.py:513
  230.5 0.0 reduce-scatter.2.cloned.1.call-update
  230.5 45.9 %reduce-scatter.2.cloned.1.call-done = bf16[256,1344]{0,1:T(8,128)(2,1)} async-done(((bf16[256,5376]{0,1:T(8,128)(2,1)}), bf16[256,1344]{0,1:T(8,128)(2,1)}) %reduce-scatter.2.cloned.1.call-update) | async-done | bytes 688144 | tf_op jit(solution)/shard_map/reduce_scatter | solution.py:514
  (26 shorter events, 0.1 us)
Async XLA Ops:
  7.2 60.2 %copy-start = (bf16[256,5376]{1,0:T(8,128)(2,1)S(1)}, bf16[256,5376]{1,0:T(8,128)(2,1)}, u32[]{:S(2)}) copy-start(bf16[256,5376]{1,0:T(8,128)(2,1)} %param.10) | copy-start | bytes 8257540
  7.2 269.3 %reduce-scatter.2.cloned.1.call-start = ((), (), s32[]{:S(2)}) async-start(), calls=%async_computation.1 | async-start | bytes 3440640 | tf_op jit(solution)/shard_map/reduce_scatter | solution.py:514
  67.4 4.2 %copy-start.22 = (f32[256,64]{1,0:T(8,128)S(1)}, f32[256,64]{1,0:T(8,128)}, u32[]{:S(2)}) copy-start(f32[256,64]{1,0:T(8,128)} %get-tuple-element.20) | copy-start | bytes 196612
  67.4 4.3 %copy-start.18 = (f32[128]{0:T(128)S(1)}, f32[128]{0:T(128)}, u32[]{:S(2)}) copy-start(f32[128]{0:T(128)} %param.15) | copy-start | bytes 1540
  72.1 0.7 copy-start.2
  72.8 0.7 copy-start.4
  73.5 0.6 copy-start.7
  165.4 9.9 %copy-start.3 = (bf16[256,512]{1,0:T(8,128)(2,1)S(1)}, bf16[256,512]{1,0:T(8,128)(2,1)}, u32[]{:S(2)}) copy-start(bf16[256,512]{1,0:T(8,128)(2,1)} %copy-done.2) | copy-start | bytes 786436
  165.4 9.8 %copy-start.19 = (s32[4]{0:T(128)S(1)}, s32[4]{0:T(128)}, u32[]{:S(2)}) copy-start(s32[4]{0:T(128)} %windows_ref.1) | copy-start | bytes 52
  165.4 9.8 %copy-start.20 = (f32[128]{0:T(128)S(1)}, f32[128]{0:T(128)}, u32[]{:S(2)}) copy-start(f32[128]{0:T(128)} %param.14) | copy-start | bytes 1540
  175.2 0.9 copy-start.5
  176.1 0.9 copy-start.8
  177.0 1.2 copy-start.10
  178.3 1.0 copy-start.13
  179.3 0.9 copy-start.16
  180.2 0.9 copy-start.17
  181.2 0.6 copy-start.21
  193.2 1.0 copy-start.11
  194.2 0.7 copy-start.12
  194.9 0.8 copy-start.14
  221.8 5.6 %slice-start = ((s8[5505024]{0:T(1024)(128)(4,1)}), s8[4194304]{0:T(1024)(128)(4,1)S(1)}, s32[]{:S(2)}) async-start(s8[5505024]{0:T(1024)(128)(4,1)} %bitcast.21), calls=%async_computation.2 | async-start | bytes 8388608
  221.8 4.5 %copy-start.1 = (bf16[4,256,512]{2,1,0:T(8,128)(2,1)S(1)}, bf16[4,256,512]{2,1,0:T(8,128)(2,1)}, u32[]{:S(2)}) copy-start(bf16[4,256,512]{2,1,0:T(8,128)(2,1)} %shard_map.117.near_ref) | copy-start | bytes 3145732
  221.8 4.5 %copy-start.6 = (f32[256,128]{1,0:T(8,128)S(1)}, f32[256,128]{1,0:T(8,128)}, u32[]{:S(2)}) copy-start(f32[256,128]{1,0:T(8,128)} %copy-done.4) | copy-start | bytes 393220
  221.8 4.5 %copy-start.9 = (f32[256,128]{1,0:T(8,128)S(1)}, f32[256,128]{1,0:T(8,128)}, u32[]{:S(2)}) copy-start(f32[256,128]{1,0:T(8,128)} %copy-done.7) | copy-start | bytes 393220
  221.8 4.5 %copy-start.15 = (f32[256,512]{1,0:T(8,128)S(1)}, f32[256,512]{1,0:T(8,128)}, u32[]{:S(2)}) copy-start(f32[256,512]{1,0:T(8,128)} %copy-done.14) | copy-start | bytes 1572868
  221.8 5.5 %slice-start.1 = ((s8[5505024]{0:T(1024)(128)(4,1)}), s8[1310720]{0:T(1024)(128)(4,1)S(1)}, s32[]{:S(2)}) async-start(s8[5505024]{0:T(1024)(128)(4,1)} %bitcast.21), calls=%async_computation.3 | async-start | bytes 2621440
Sparse Core Ops, SparseCore 0:
  230.6 45.7 reduce-scatter.1

commit v2 on v1

--- a/solution.py
+++ b/solution.py
@@ -29,7 +29,7 @@
     return [(a, b - a) for a, b in zip(edges, edges[1:])]
 
 
-def ring_gather(n, jobs, me, send_sems, recv_sems, middle=None):
+def ring_gather(n, jobs, me, send_sems, recv_sems, middle, later=None):
     place = ring_place(me, n)
 
     def at(distance):
@@ -60,8 +60,7 @@
 
     for job in range(len(jobs)):
         first(job).start()
-    if middle is not None:
-        middle()
+    middle()
 
     def arrived(step, job):
         source, dest, way = jobs[job]
@@ -81,7 +80,11 @@
             copy(step, job).start()
         return carry
 
-    lax.fori_loop(1, n - 1, body, 0)
+    turn = n // 2 - 1
+    lax.fori_loop(1, turn, body, 0)
+    if later is not None:
+        later()
+    lax.fori_loop(turn, n - 1, body, 0)
     for job in range(len(jobs)):
         arrived(n - 2, job).wait_recv()
 
@@ -100,16 +103,38 @@
     pl.semaphore_wait(barrier, len(peers))
 
 
-def greet_near(n, me, reach):
+def greet_near(n, me):
     barrier = pltpu.get_barrier_semaphore()
-    for step in range(1, reach + 1):
-        for peer, there in ((me + step, me + step < n), (me - step, me >= step)):
-
-            @pl.when(there)
-            def _():
-                pl.semaphore_signal(barrier, inc=1, device_id={"seq": peer}, device_id_type=MESH)
-
-    pl.semaphore_wait(barrier, jnp.minimum(me, reach) + jnp.minimum(n - 1 - me, reach))
+
+    def signal(peer):
+        pl.semaphore_signal(barrier, inc=1, device_id={"seq": peer}, device_id_type=MESH)
+
+    signal(pair_of(me))
+
+    @pl.when(me + 2 < n)
+    def _():
+        signal(me + 2)
+
+    @pl.when(me >= 2)
+    def _():
+        signal(me - 2)
+
+    pl.semaphore_wait(barrier, 1 + jnp.minimum(me // 2, 1) + jnp.minimum((n - 1 - me) // 2, 1))
+
+
+def pair_of(me):
+    return me + 1 - 2 * (me % 2)
+
+
+def to_seq(source, dest, peer, send, recv):
+    return pltpu.make_async_remote_copy(
+        src_ref=source,
+        dst_ref=dest,
+        send_sem=send,
+        recv_sem=recv,
+        device_id={"seq": peer},
+        device_id_type=MESH,
+    )
 
 
 def kv_gather_kernel(n, k_ref, v_ref, tile_ref, kv_out, tile_out, send, recv, local):
@@ -170,47 +195,22 @@
     )(k_weight, v_weight, tile)
 
 
-def near_copies(n, me, reach, way, source, dest, send, recv):
-    result = []
-    for step in range(reach, 0, -1):
-        peer = me + way * step
-        goes = peer < n if way > 0 else peer >= 0
-        back = me - way * step
-        comes = back >= 0 if way > 0 else back < n
-        copy = pltpu.make_async_remote_copy(
-            src_ref=source(step),
-            dst_ref=dest(step),
-            send_sem=send.at[step - 1],
-            recv_sem=recv.at[step - 1],
-            device_id={"seq": peer},
-            device_id_type=MESH,
-        )
-        result.append((copy, goes, comes))
-    return result
-
-
-def start_near(copies):
-    for copy, goes, _ in copies:
-        pl.when(goes)(copy.start)
-
-
-def finish_near(copies):
-    for copy, goes, comes in copies:
-        pl.when(goes)(copy.wait_send)
-        pl.when(comes)(copy.wait_recv)
-
-
-def q_gather_kernel(n, reach, q_ref, kv_ref, q_out, near_out, send, recv, nsend, nrecv, local):
+def q_gather_kernel(n, q_ref, kv_ref, q_out, near_out, send, recv, nsend, nrecv, local):
     me = lax.axis_index("seq")
+    odd = me % 2
     rows = q_ref.shape[0]
-    greet_near(n, me, reach)
+    greet_near(n, me)
     own = pltpu.make_async_copy(q_ref, q_out.at[me], local.at[0])
-    copies = near_copies(
-        n, me, reach, 1, lambda step: kv_ref, lambda step: near_out.at[step - 1], nsend, nrecv
-    )
-    cuts = row_cuts(rows, 4)
+    pair = pair_of(me)
+    up = to_seq(kv_ref, near_out.at[1], me + 2, nsend.at[0], nrecv.at[1])
+    across = to_seq(kv_ref, near_out.at[0], pair, nsend.at[1], nrecv.at[0])
+    up_again = to_seq(near_out.at[1], near_out.at[3], me + 2, nsend.at[2], nrecv.at[3])
+    slot = 2 - 2 * odd
+    across_two = to_seq(near_out.at[1], near_out.at[slot], pair, nsend.at[3], nrecv.at[slot])
+    across_four = to_seq(near_out.at[3], near_out.at[2], pair, nsend.at[4], nrecv.at[2])
+    has_up = me + 2 < n
     jobs = []
-    for i, (a, size) in enumerate(cuts):
+    for i, (a, size) in enumerate(row_cuts(rows, 4)):
         jobs.append(
             (
                 q_ref.at[pl.ds(a, size)],
@@ -219,10 +219,45 @@
             )
         )
 
-    start_near(copies)
-    ring_gather(n, jobs, me, send, recv, own.start)
+    pl.when(has_up)(up.start)
+    pl.when(odd == 0)(across.start)
+
+    def middle():
+        own.start()
+
+        @pl.when(me >= 2)
+        def _():
+            up.wait_recv()
+            across_two.start()
+            pl.when(has_up)(up_again.start)
+
+    def later():
+        @pl.when(me >= 4)
+        def _():
+            up_again.wait_recv()
+            pl.when(odd == 1)(across_four.start)
+
+    ring_gather(n, jobs, me, send, recv, middle, later)
     own.wait()
-    finish_near(copies)
+
+    @pl.when(has_up)
+    def _():
+        up.wait_send()
+        pl.when(me >= 2)(up_again.wait_send)
+
+    pl.when(me >= 2)(across_two.wait_send)
+
+    @pl.when(odd == 0)
+    def _():
+        across.wait_send()
+        pl.when(me >= 2)(lambda: to_seq(kv_ref, near_out.at[0], pair, nsend.at[1], nrecv.at[0]).wait_recv())
+        pl.when(me >= 4)(across_four.wait_recv)
+
+    @pl.when(odd == 1)
+    def _():
+        across.wait_recv()
+        pl.when(me >= 4)(across_four.wait_send)
+        pl.when(me >= 2)(lambda: to_seq(kv_ref, near_out.at[2], pair, nsend.at[1], nrecv.at[2]).wait_recv())
 
 
 def q_gather(n, reach, q_weight, kv_own):
@@ -230,7 +265,7 @@
     jobs = len(row_cuts(rows, 4))
     hbm = pl.BlockSpec(memory_space=pl.ANY)
     return pl.pallas_call(
-        functools.partial(q_gather_kernel, n, reach),
+        functools.partial(q_gather_kernel, n),
         out_shape=[
             jax.ShapeDtypeStruct((n, rows, width), jnp.bfloat16),
             jax.ShapeDtypeStruct((reach,) + kv_own.shape, jnp.bfloat16),
@@ -240,7 +275,7 @@
         scratch_shapes=[
             pltpu.SemaphoreType.DMA((n - 1, jobs)),
             pltpu.SemaphoreType.DMA((n - 1, jobs)),
-            pltpu.SemaphoreType.DMA((reach,)),
+            pltpu.SemaphoreType.DMA((5,)),
             pltpu.SemaphoreType.DMA((reach,)),
             pltpu.SemaphoreType.DMA((1,)),
         ],
@@ -248,36 +283,195 @@
     )(q_weight, kv_own)
 
 
-def give_back_kernel(n, reach, near_ref, near_out, send, recv):
+CUTS = 4
+
+
+def give_back_kernel(n, near_ref, down_ref, total_ref, beside, other, far_in, far, mid, mid_in, send, recv):
     me = lax.axis_index("seq")
-    greet_near(n, me, reach)
-    copies = near_copies(
-        n,
-        me,
-        reach,
-        -1,
-        lambda step: near_ref.at[step - 1],
-        lambda step: near_out.at[step - 1],
-        send,
-        recv,
-    )
-    start_near(copies)
-    finish_near(copies)
-
-
-def give_back(n, reach, near):
-    hbm = pl.BlockSpec(memory_space=pl.ANY)
+    odd = me % 2
+    pair = pair_of(me)
+    size = near_ref.shape[1] // CUTS
+    f32 = jnp.float32
+    greet_near(n, me)
+
+    def rows(i):
+        return pl.ds(pl.multiple_of(i * size, size), size)
+
+    def copies(i):
+        r = rows(i)
+        return (
+            to_seq(near_ref.at[2 - 2 * odd, r], other.at[r], pair, send.at[0, i], recv.at[0, i]),
+            to_seq(near_ref.at[2 * odd, r], beside.at[r], pair, send.at[1, i], recv.at[1, i]),
+            to_seq(far.at[r], far_in.at[r], me - 2, send.at[2, i], recv.at[2, i]),
+            to_seq(mid.at[r], mid_in.at[r], me - 2, send.at[3, i], recv.at[3, i]),
+        )
+
+    def loop(step):
+        lax.fori_loop(0, CUTS, lambda i, c: (step(i), c)[1], 0)
+
+    def begin(i):
+        a, b, _, _ = copies(i)
+        a.start()
+        b.start()
+
+    loop(begin)
+
+    def send_far(i):
+        a, _, c, _ = copies(i)
+        r = rows(i)
+        far[r] = near_ref[3, r]
+
+        @pl.when(odd == 1)
+        def _():
+            a.wait_recv()
+            far[r] = (near_ref[3, r].astype(f32) + other[r].astype(f32)).astype(jnp.bfloat16)
+
+        pl.when(me >= 2)(c.start)
+
+    loop(send_far)
+
+    def send_mid(i):
+        _, b, c, d = copies(i)
+        r = rows(i)
+        b.wait_recv()
+        mid[r] = (near_ref[1, r].astype(f32) + beside[r].astype(f32)).astype(jnp.bfloat16)
+
+        @pl.when(me + 2 < n)
+        def _():
+            c.wait_recv()
+            mid[r] = (
+                near_ref[1, r].astype(f32) + beside[r].astype(f32) + far_in[r].astype(f32)
+            ).astype(jnp.bfloat16)
+
+        pl.when(me >= 2)(d.start)
+
+    loop(send_mid)
+
+    def finish(i):
+        a, b, c, d = copies(i)
+        r = rows(i)
+        total_ref[r] = down_ref[r]
+
+        @pl.when(odd == 0)
+        def _():
+            a.wait_recv()
+            total_ref[r] = down_ref[r] + other[r].astype(f32)
+
+        @pl.when(me + 2 < n)
+        def _():
+            d.wait_recv()
+            total_ref[r] = total_ref[r] + mid_in[r].astype(f32)
+
+        a.wait_send()
+        b.wait_send()
+
+        @pl.when(me >= 2)
+        def _():
+            c.wait_send()
+            d.wait_send()
+
+    loop(finish)
+
+
+def give_back(n, near, down):
     return pl.pallas_call(
-        functools.partial(give_back_kernel, n, reach),
-        out_shape=jax.ShapeDtypeStruct(near.shape, jnp.bfloat16),
-        in_specs=[hbm],
-        out_specs=hbm,
+        functools.partial(give_back_kernel, n),
+        out_shape=jax.ShapeDtypeStruct(down.shape, jnp.float32),
+        in_specs=[VMEM] * 2,
+        out_specs=VMEM,
+        scratch_shapes=[pltpu.VMEM(down.shape, jnp.bfloat16)] * 6
+        + [pltpu.SemaphoreType.DMA((4, CUTS))] * 2,
+        compiler_params=pltpu.CompilerParams(
+            collective_id=2, has_side_effects=True, vmem_limit_bytes=40 * 1024 * 1024
+        ),
+    )(near, down)
+
+
+def head_sum_kernel(part_ref, out_ref, from_core, stage, from_y, send, recv):
+    h = lax.axis_index("head")
+    core, y = h % 2, h // 2
+    size = out_ref.shape[0] // CUTS
+    f32 = jnp.float32
+    mate = 2 * y + 1 - core
+    across = 2 * (1 - y) + core
+    barrier = pltpu.get_barrier_semaphore()
+    for peer in (mate, across):
+        pl.semaphore_signal(barrier, inc=1, device_id={"head": peer}, device_id_type=MESH)
+    pl.semaphore_wait(barrier, 2)
+
+    def rows(i):
+        return pl.ds(pl.multiple_of(i * size, size), size)
+
+    def to_head(source, dest, peer, kind, i):
+        return pltpu.make_async_remote_copy(
+            src_ref=source,
+            dst_ref=dest,
+            send_sem=send.at[kind, i],
+            recv_sem=recv.at[kind, i],
+            device_id={"head": peer},
+            device_id_type=MESH,
+        )
+
+    def copies(i):
+        r = rows(i)
+        return (
+            to_head(part_ref.at[2 * (1 - y) + 1 - core, r], from_core.at[0, r], mate, 0, i),
+            to_head(part_ref.at[2 * y + 1 - core, r], from_core.at[1, r], mate, 1, i),
+            to_head(stage.at[r], from_y.at[r], across, 2, i),
+        )
+
+    def loop(step):
+        lax.fori_loop(0, CUTS, lambda i, c: (step(i), c)[1], 0)
+
+    loop(lambda i: copies(i)[0].start())
+    loop(lambda i: copies(i)[1].start())
+
+    def pass_on(i):
+        a, _, c = copies(i)
+        r = rows(i)
+        a.wait_recv()
+        stage[r] = (
+            part_ref[2 * (1 - y) + core, r].astype(f32) + from_core[0, r].astype(f32)
+        ).astype(jnp.bfloat16)
+        c.start()
+
+    loop(pass_on)
+
+    def finish(i):
+        a, b, c = copies(i)
+        r = rows(i)
+        b.wait_recv()
+        c.wait_recv()
+        out_ref[r] = (
+            part_ref[2 * y + core, r].astype(f32)
+            + from_core[1, r].astype(f32)
+            + from_y[r].astype(f32)
+        ).astype(jnp.bfloat16)
+        a.wait_send()
+        b.wait_send()
+        c.wait_send()
+
+    loop(finish)
+
+
+def head_sum(parts):
+    block = parts.shape[1:]
+    return pl.pallas_call(
+        head_sum_kernel,
+        out_shape=jax.ShapeDtypeStruct(block, jnp.bfloat16),
+        in_specs=[VMEM],
+        out_specs=VMEM,
         scratch_shapes=[
-            pltpu.SemaphoreType.DMA((reach,)),
-            pltpu.SemaphoreType.DMA((reach,)),
+            pltpu.VMEM((2,) + block, jnp.bfloat16),
+            pltpu.VMEM(block, jnp.bfloat16),
+            pltpu.VMEM(block, jnp.bfloat16),
+            pltpu.SemaphoreType.DMA((3, CUTS)),
+            pltpu.SemaphoreType.DMA((3, CUTS)),
         ],
-        compiler_params=pltpu.CompilerParams(collective_id=2, has_side_effects=True),
-    )(near)
+        compiler_params=pltpu.CompilerParams(
+            collective_id=3, has_side_effects=True, vmem_limit_bytes=40 * 1024 * 1024
+        ),
+    )(parts)
 
 
 def swap_halves(x):
@@ -297,7 +491,9 @@
     return r * dn - u * (r * r * r) * jnp.mean(u * dn, axis=-1, keepdims=True)
 
 
-def kv_ready_kernel(lin_ref, gain_ref, cos_ref, sin_ref, out_ref):
+def kv_ready_kernel(
+    tokens_total, lin_ref, gain_ref, cos_ref, sin_ref, tiles_ref, kept_ref, grad_ref, out_ref, cot_ref
+):
     width = gain_ref.shape[1]
     half = lin_ref.shape[1] // 2
     for g in range(half // width):
@@ -306,23 +502,33 @@
             lin_ref[:, cols], gain_ref[...], cos_ref[...], sin_ref[...]
         ).astype(jnp.bfloat16)
     out_ref[:, half:] = lin_ref[:, half:].astype(jnp.bfloat16)
-
-
-def kv_back_kernel(reach, own_ref, near_ref, there_ref, lin_ref, gain_ref, cos_ref, sin_ref, out_ref):
+    normalizer = jnp.sum(tiles_ref[...], axis=0)[0:1, 0:1]
+    factor = kept_ref[...] * (tokens_total / normalizer)
+    cot_ref[...] = (grad_ref[...].astype(jnp.float32) * factor).astype(jnp.bfloat16)
+
+
+def back_kernel(
+    total_ref, lin_ref, gain_ref, cos_ref, sin_ref, dq_ref, q_mat, kv_mat, out_ref, dkv
+):
     width = gain_ref.shape[1]
     full = lin_ref.shape[1]
     half = full // 2
-    for g in range(full // width):
+    for g in range(half // width):
         cols = slice(g * width, (g + 1) * width)
-        total = own_ref[:, cols]
-        for step in range(reach):
-            part = near_ref[step, :, cols].astype(jnp.float32)
-            total = total + jnp.where(there_ref[step] > 0, part, 0.0)
-        if g * width < half:
-            total = rotate_back(
-                lin_ref[:, cols], gain_ref[...], cos_ref[...], sin_ref[...], total
-            )
-        out_ref[:, cols] = total.astype(jnp.bfloat16)
+        dkv[:, cols] = rotate_back(
+            lin_ref[:, cols], gain_ref[...], cos_ref[...], sin_ref[...], total_ref[:, cols]
+        ).astype(jnp.bfloat16)
+    dkv[:, half:] = total_ref[:, half:].astype(jnp.bfloat16)
+    last = (((1,), (1,)), ((), ()))
+
+    def quarter(i, carry):
+        out_ref[i] = (
+            lax.dot_general(dq_ref[...], q_mat[i], last, preferred_element_type=jnp.float32)
+            + lax.dot_general(dkv[...], kv_mat[i], last, preferred_element_type=jnp.float32)
+        ).astype(jnp.bfloat16)
+        return carry
+
+    lax.fori_loop(0, out_ref.shape[0], quarter, 0)
 
 
 def attend_kernel(
@@ -334,8 +540,7 @@
     lin_ref,
     own_ref,
     near_ref,
-    grad_ref,
-    factor_ref,
+    cot_ref,
     gain_ref,
     cos_ref,
     sin_ref,
@@ -367,7 +572,7 @@
         vcols = pl.ds(pl.multiple_of((kv_heads + h // group) * width, width), width)
         u = lin_ref[:, cols]
         q = rotate(u, gain_ref[...], cos_ref[...], sin_ref[...]).astype(jnp.bfloat16)
-        cot = (grad_ref[:, cols].astype(jnp.float32) * factor_ref[...]).astype(jnp.bfloat16)
+        cot = cot_ref[:, cols]
         peak = jnp.full((rows, 1), -1e30, jnp.float32)
         for b in range(reach + 1):
             s = scale * lax.dot_general(
@@ -454,9 +659,6 @@
     kept = token_weight * loss_mask.astype(f32)
     tile = jnp.broadcast_to(jnp.sum(kept), (8, 128))
     kv_full, tiles = kv_gather(n, k_weight, v_weight, tile)
-    normalizer = jnp.sum(tiles[:, 0, 0])
-    factor = (kept * (tok_rows * n / normalizer))[:, None]
-
     positions = me * tok_rows + jnp.arange(tok_rows, dtype=jnp.int32)
     half_width = head_width // 2
     frequency = 10000.0 ** (-(jnp.arange(half_width, dtype=f32) * 2.0) / head_width)
@@ -466,19 +668,21 @@
     sine = jnp.concatenate([-sine, sine], axis=1)
     steps = jnp.arange(1, reach + 1, dtype=jnp.int32)
     before = (me >= steps).astype(jnp.int32)
-    after = (me + steps < n).astype(jnp.int32)
     q_gain = q_gain[None, :]
     k_gain = k_gain[None, :]
 
     kv_matrix = kv_full.reshape(depth, kv_cols)
     kv_lin = jnp.dot(tokens, kv_matrix, preferred_element_type=f32)
-    kv_own = pl.pallas_call(
-        kv_ready_kernel,
-        out_shape=jax.ShapeDtypeStruct((tok_rows, kv_cols), jnp.bfloat16),
-        in_specs=[VMEM] * 4,
-        out_specs=VMEM,
+    kv_own, cot = pl.pallas_call(
+        functools.partial(kv_ready_kernel, float(tok_rows * n)),
+        out_shape=[
+            jax.ShapeDtypeStruct((tok_rows, kv_cols), jnp.bfloat16),
+            jax.ShapeDtypeStruct((tok_rows, q_cols), jnp.bfloat16),
+        ],
+        in_specs=[VMEM] * 7,
+        out_specs=[VMEM] * 2,
         compiler_params=ROOM,
-    )(kv_lin, k_gain, cosine, sine)
+    )(kv_lin, k_gain, cosine, sine, tiles, kept[:, None], grad_attn)
     q_full, near = q_gather(n, reach, q_weight, kv_own)
     q_matrix = q_full.reshape(depth, q_cols)
     q_lin = jnp.dot(tokens, q_matrix, preferred_element_type=f32)
@@ -490,7 +694,7 @@
             jax.ShapeDtypeStruct((tok_rows, kv_cols), f32),
             jax.ShapeDtypeStruct((reach, tok_rows, kv_cols), jnp.bfloat16),
         ],
-        in_specs=[SMEM] * 2 + [VMEM] * 8,
+        in_specs=[SMEM] * 2 + [VMEM] * 7,
         out_specs=[VMEM] * 4,
         scratch_shapes=[
             pltpu.VMEM((reach + 1, tok_rows, kv_cols), jnp.bfloat16),
@@ -498,22 +702,27 @@
             pltpu.VMEM((reach + 1, tok_rows, kv_cols), f32),
         ],
         compiler_params=ROOM,
-    )(before, windows, q_lin, kv_own, near, grad_attn, factor, q_gain, cosine, sine)
-    returned = give_back(n, reach, dnear)
-    dkv_lin = pl.pallas_call(
-        functools.partial(kv_back_kernel, reach),
-        out_shape=jax.ShapeDtypeStruct((tok_rows, kv_cols), jnp.bfloat16),
-        in_specs=[VMEM, VMEM, SMEM] + [VMEM] * 4,
+    )(before, windows, q_lin, kv_own, near, cot, q_gain, cosine, sine)
+    total = give_back(n, dnear, down)
+    heads = lax.axis_size("head")
+    parts = pl.pallas_call(
+        back_kernel,
+        out_shape=jax.ShapeDtypeStruct((heads, tok_rows, depth // heads), jnp.bfloat16),
+        in_specs=[VMEM] * 8,
         out_specs=VMEM,
+        scratch_shapes=[pltpu.VMEM((tok_rows, kv_cols), jnp.bfloat16)],
         compiler_params=ROOM,
-    )(down, returned, after, kv_lin, k_gain, cosine, sine)
-    contract = (((1,), (1,)), ((), ()))
-    partial_grad = lax.dot_general(
-        dq_lin, q_matrix, contract, preferred_element_type=f32
-    ) + lax.dot_general(dkv_lin, kv_matrix, contract, preferred_element_type=f32)
-    grad_tokens = lax.psum_scatter(
-        partial_grad.astype(jnp.bfloat16), "head", scatter_dimension=1, tiled=True
+    )(
+        total,
+        kv_lin,
+        k_gain,
+        cosine,
+        sine,
+        dq_lin,
+        q_full.reshape(heads, depth // heads, q_cols),
+        kv_full.reshape(heads, depth // heads, kv_cols),
     )
+    grad_tokens = head_sum(parts)
     return (attended, grad_tokens)
 
 

time: 285 us -> 202 us (0.71)
  waiting for transfers between devices: 45.9 us -> 0 us
  between operations: 15 us -> 0.94 us
  local copies, waits for them, and re-layouts: 13.8 us -> 4.62 us
  matrix products: 16.7 us -> 8.46 us
  other arithmetic: 5.94 us -> 2.14 us
  Pallas kernels: 186 us -> 183 us
    reduce_scatter x1 -> x0, waiting for transfers between devices: 45.9 us -> none  [body(): lax.psum_scatter(partial_grad.astype(jnp.bfloat16), 'head', scatter_dimen...]
    unnamed x50 -> x29, local copies, waits for them, and re-layouts: 11.1 us -> 2.58 us
    dot_general x2 -> x0, matrix products: 7.58 us -> none  [the longest x1 4.42 us: body(): lax.dot_general(dq_lin, q_matrix, contract, preferred_element_type=f32)]
    pallas_call x4 -> x5, Pallas kernels: 119 us -> 116 us  [the longest x1 67.8 us: q_gather(): pl.pallas_call(functools.partial(q_gather_kernel, n), out_shape=[jax.Shap...]
  transfers between devices with their start and end apart: 1 -> 0, of which waited for: 1 -> 0; matrix products, arithmetic and copies ran while one was open for 0% -> 0% of each run, Pallas kernels for 0% -> 0%
where the time goes in v2:
time: 202 us; the launch traced here: 199 us
  Pallas kernels  183 us (91%)
  matrix products  8.46 us (4%)
  local copies, waits for them, and re-layouts  4.62 us (2%)
  other arithmetic  2.14 us (1%)
    pallas_call x1, Pallas kernels, q_gather(): pl.pallas_call(functools.partial(q_gather_kernel, n), out_shape=[jax.Shap...  67.8 us
    pallas_call x1, Pallas kernels, kv_gather(): pl.pallas_call(functools.partial(kv_gather_kernel, n), out_shape=[jax.Sha...  55.8 us
    pallas_call x1, Pallas kernels, give_back(): pl.pallas_call(functools.partial(give_back_kernel, n), out_shape=jax.Shap...  20.4 us
    pallas_call x1, Pallas kernels, head_sum(): pl.pallas_call(head_sum_kernel, out_shape=jax.ShapeDtypeStruct(block, jnp...  20.1 us
    pallas_call x1, Pallas kernels, body(): pl.pallas_call(functools.partial(attend_kernel, reach, kv_heads, scale),...  11.3 us
    pallas_call x1, Pallas kernels, body(): pl.pallas_call(back_kernel, out_shape=jax.ShapeDtypeStruct((heads, tok_ro...  6.99 us
    dot_general x1, matrix products, body(): q_lin = jnp.dot(tokens, q_matrix, preferred_element_type=f32)  4.28 us
    dot_general x1, matrix products, body(): kv_lin = jnp.dot(tokens, kv_matrix, preferred_element_type=f32)  4.18 us

profile of v2, /device:TPU:18, one launch (start us, length us, event | category | flops | bytes accessed | tf_op | source)
XLA Modules:
  0.0 199.1 jit_solution(3220539196111876211)
XLA Ops:
  0.6 0.0 copy-start
  0.7 1.5 fusion.1
  2.1 1.2 broadcast_in_dim.14.tile_ref
  3.4 0.8 copy.16.kept_ref
  4.2 0.5 fusion
  4.7 0.1 pad_maximum_fusion
  4.9 55.8 %shard_map.113 = (bf16[8,672,512]{2,1,0:T(8,128)(2,1)}, f32[8,8,128]{2,1,0:T(8,128)}) custom-call(bf16[672,256]{1,0:T(8,128)(2,1)} %k_ref.1, bf16[672,256]{1,0:T(8,128)(2,1)} %v_ref.1, f32[8,128]{1,0:T(8,128)} %broadcast_in_dim.14.tile_ref), custom_call_target="tpu_custom_call" | custom-call | tf_op jit(solution)/shard_map/pallas_call | solution.py:181
  60.7 0.0 copy-done
  60.7 0.0 copy-start.4
  60.7 0.0 copy-start.7
  60.7 0.0 copy-start.8
  60.7 0.0 copy-start.9
  60.8 4.2 %convolution_bitcast_fusion.1.lin_ref = f32[256,512]{1,0:T(8,128)S(1)} fusion(bf16[256,5376]{1,0:T(8,128)(2,1)S(1)} %copy-done, bf16[5376,512]{1,0:T(8,128)(2,1)} %bitcast.22), kind=kOutput, calls=%fused_computation.1 | convolution fusion | flops 1409286144 | bytes 8781824 | tf_op jit(solution)/shard_map/dot_general | solution.py:675
  64.9 0.0 copy-done.4
  65.0 0.0 copy-done.7
  65.0 0.0 copy-done.8
  65.0 0.0 copy-done.9
  65.0 0.4 shard_map.114
  65.4 0.0 copy-start.2
  65.4 0.7 copy-done.2
  66.1 0.0 copy-start.5
  66.1 0.7 copy-done.5
  66.8 67.8 %shard_map.115 = (bf16[8,672,512]{2,1,0:T(8,128)(2,1)}, bf16[4,256,512]{2,1,0:T(8,128)(2,1)}) custom-call(bf16[672,512]{1,0:T(8,128)(2,1)} %q_ref.1, bf16[256,512]{1,0:T(8,128)(2,1)} %copy-done.2), custom_call_target="tpu_custom_call" | custom-call | tf_op jit(solution)/shard_map/pallas_call | solution.py:267
  134.6 0.0 slice-start
  134.6 0.0 copy-start.1
  134.6 0.0 copy-start.3
  134.6 0.0 copy-start.6
  134.7 0.0 copy-start.10
  134.7 0.0 copy-start.11
  134.7 0.0 slice-start.1
  134.7 4.3 %convolution_bitcast_fusion.lin_ref = f32[256,512]{1,0:T(8,128)S(1)} fusion(bf16[256,5376]{1,0:T(8,128)(2,1)S(1)} %copy-done, bf16[5376,512]{1,0:T(8,128)(2,1)} %bitcast.15), kind=kOutput, calls=%fused_computation | convolution fusion | flops 1409286144 | bytes 8781824 | tf_op jit(solution)/shard_map/dot_general | solution.py:688
  139.0 0.0 copy-done.1
  139.0 0.0 copy-done.3
  139.0 0.0 copy-done.6
  139.0 0.0 copy-done.10
  139.0 0.0 copy-done.11
  139.0 11.3 %shard_map.116 = (bf16[256,512]{1,0:T(8,128)(2,1)}, bf16[256,512]{1,0:T(8,128)(2,1)S(1)}, f32[256,512]{1,0:T(8,128)S(1)}, bf16[4,256,512]{2,1,0:T(8,128)(2,1)S(1)}) custom-call(s32[4]{0:T(128)S(1)} %compare_convert_fusion.there_ref, s32[4]{0:T(128)S(1)} %copy-done.10, f32[256,512]{1,0:T(8,128)S(1)} %convolution_bitcast_fusion.lin_ref, ...), custom_call_target="tpu_custom_call" | custom-call | tf_op jit(solution)/shard_map/pallas_call | solution.py:689
  150.4 20.4 %shard_map.117.total_ref = f32[256,512]{1,0:T(8,128)S(1)} custom-call(bf16[4,256,512]{2,1,0:T(8,128)(2,1)S(1)} %get-tuple-element.19.near_ref, f32[256,512]{1,0:T(8,128)S(1)} %get-tuple-element.20.down_ref), custom_call_target="tpu_custom_call" | custom-call | tf_op jit(solution)/shard_map/pallas_call | solution.py:377
  170.8 0.0 slice-done
  170.8 0.0 slice-done.1
  170.8 7.0 %shard_map.118.part_ref = bf16[4,256,1344]{2,1,0:T(8,128)(2,1)S(1)} custom-call(f32[256,512]{1,0:T(8,128)S(1)} %shard_map.117.total_ref, f32[256,512]{1,0:T(8,128)S(1)} %convolution_bitcast_fusion.1.lin_ref, f32[1,128]{1,0:T(1,128)S(1)} %bitcast.20, f32[256,128]{1,0:T(8,128)S(1)} %get-tuple-element.31.cos_ref, f32[256,128]{1,0:T(8,128)S(1)} %get-tuple-element.32.sin_ref, ...), custom_call_target="tpu_custom_call" | custom-call | tf_op jit(solution)/shard_map/pallas_call | solution.py:708
  177.8 20.1 %shard_map.119 = bf16[256,1344]{1,0:T(8,128)(2,1)S(1)} custom-call(bf16[4,256,1344]{2,1,0:T(8,128)(2,1)S(1)} %shard_map.118.part_ref), custom_call_target="tpu_custom_call" | custom-call | tf_op jit(solution)/shard_map/pallas_call | solution.py:459
  198.0 1.1 copy.18
  (4 shorter events, 0.0 us)
Async XLA Ops:
  0.6 60.1 %copy-start = (bf16[256,5376]{1,0:T(8,128)(2,1)S(1)}, bf16[256,5376]{1,0:T(8,128)(2,1)}, u32[]{:S(2)}) copy-start(bf16[256,5376]{1,0:T(8,128)(2,1)} %param.10) | copy-start | bytes 8257540
  60.7 4.2 %copy-start.4 = (f32[256,1]{1,0:T(8,128)S(1)}, f32[256,1]{1,0:T(8,128)}, u32[]{:S(2)}) copy-start(f32[256,1]{1,0:T(8,128)} %copy.16.kept_ref) | copy-start | bytes 3076
  60.7 4.2 %copy-start.7 = (bf16[256,512]{1,0:T(8,128)(2,1)S(1)}, bf16[256,512]{1,0:T(8,128)(2,1)}, u32[]{:S(2)}) copy-start(bf16[256,512]{1,0:T(8,128)(2,1)} %grad_ref.1) | copy-start | bytes 786436
  60.7 4.2 %copy-start.8 = (f32[8,8,128]{2,1,0:T(8,128)S(1)}, f32[8,8,128]{2,1,0:T(8,128)}, u32[]{:S(2)}) copy-start(f32[8,8,128]{2,1,0:T(8,128)} %get-tuple-element.13.tiles_ref) | copy-start | bytes 98308
  60.7 4.2 %copy-start.9 = (f32[128]{0:T(128)S(1)}, f32[128]{0:T(128)}, u32[]{:S(2)}) copy-start(f32[128]{0:T(128)} %param.15) | copy-start | bytes 1540
  65.4 0.7 copy-start.2
  66.1 0.7 copy-start.5
  134.6 36.2 %slice-start = ((s8[5505024]{0:T(1024)(128)(4,1)}), s8[4194304]{0:T(1024)(128)(4,1)S(1)}, s32[]{:S(2)}) async-start(s8[5505024]{0:T(1024)(128)(4,1)} %bitcast.16), calls=%async_computation | async-start | bytes 8388608
  134.6 4.4 %copy-start.1 = (bf16[4,256,512]{2,1,0:T(8,128)(2,1)S(1)}, bf16[4,256,512]{2,1,0:T(8,128)(2,1)}, u32[]{:S(2)}) copy-start(bf16[4,256,512]{2,1,0:T(8,128)(2,1)} %get-tuple-element.16.near_ref) | copy-start | bytes 3145732
  134.6 4.4 %copy-start.3 = (bf16[256,512]{1,0:T(8,128)(2,1)S(1)}, bf16[256,512]{1,0:T(8,128)(2,1)}, u32[]{:S(2)}) copy-start(bf16[256,512]{1,0:T(8,128)(2,1)} %copy-done.2) | copy-start | bytes 786436
  134.6 4.4 %copy-start.6 = (bf16[256,512]{1,0:T(8,128)(2,1)S(1)}, bf16[256,512]{1,0:T(8,128)(2,1)}, u32[]{:S(2)}) copy-start(bf16[256,512]{1,0:T(8,128)(2,1)} %copy-done.5) | copy-start | bytes 786436
  134.7 4.4 %copy-start.10 = (s32[4]{0:T(128)S(1)}, s32[4]{0:T(128)}, u32[]{:S(2)}) copy-start(s32[4]{0:T(128)} %windows_ref.1) | copy-start | bytes 52
  134.7 4.4 %copy-start.11 = (f32[128]{0:T(128)S(1)}, f32[128]{0:T(128)}, u32[]{:S(2)}) copy-start(f32[128]{0:T(128)} %param.14) | copy-start | bytes 1540
  134.7 36.1 %slice-start.1 = ((s8[5505024]{0:T(1024)(128)(4,1)}), s8[1310720]{0:T(1024)(128)(4,1)S(1)}, s32[]{:S(2)}) async-start(s8[5505024]{0:T(1024)(128)(4,1)} %bitcast.16), calls=%async_computation.1 | async-start | bytes 2621440

commit v3 on v2

--- a/solution.py
+++ b/solution.py
@@ -103,7 +103,7 @@
     pl.semaphore_wait(barrier, len(peers))
 
 
-def greet_near(n, me):
+def greet_near(n, me, more=0):
     barrier = pltpu.get_barrier_semaphore()
 
     def signal(peer):
@@ -119,7 +119,7 @@
     def _():
         signal(me - 2)
 
-    pl.semaphore_wait(barrier, 1 + jnp.minimum(me // 2, 1) + jnp.minimum((n - 1 - me) // 2, 1))
+    pl.semaphore_wait(barrier, more + 1 + jnp.minimum(me // 2, 1) + jnp.minimum((n - 1 - me) // 2, 1))
 
 
 def pair_of(me):
@@ -286,194 +286,6 @@
 CUTS = 4
 
 
-def give_back_kernel(n, near_ref, down_ref, total_ref, beside, other, far_in, far, mid, mid_in, send, recv):
-    me = lax.axis_index("seq")
-    odd = me % 2
-    pair = pair_of(me)
-    size = near_ref.shape[1] // CUTS
-    f32 = jnp.float32
-    greet_near(n, me)
-
-    def rows(i):
-        return pl.ds(pl.multiple_of(i * size, size), size)
-
-    def copies(i):
-        r = rows(i)
-        return (
-            to_seq(near_ref.at[2 - 2 * odd, r], other.at[r], pair, send.at[0, i], recv.at[0, i]),
-            to_seq(near_ref.at[2 * odd, r], beside.at[r], pair, send.at[1, i], recv.at[1, i]),
-            to_seq(far.at[r], far_in.at[r], me - 2, send.at[2, i], recv.at[2, i]),
-            to_seq(mid.at[r], mid_in.at[r], me - 2, send.at[3, i], recv.at[3, i]),
-        )
-
-    def loop(step):
-        lax.fori_loop(0, CUTS, lambda i, c: (step(i), c)[1], 0)
-
-    def begin(i):
-        a, b, _, _ = copies(i)
-        a.start()
-        b.start()
-
-    loop(begin)
-
-    def send_far(i):
-        a, _, c, _ = copies(i)
-        r = rows(i)
-        far[r] = near_ref[3, r]
-
-        @pl.when(odd == 1)
-        def _():
-            a.wait_recv()
-            far[r] = (near_ref[3, r].astype(f32) + other[r].astype(f32)).astype(jnp.bfloat16)
-
-        pl.when(me >= 2)(c.start)
-
-    loop(send_far)
-
-    def send_mid(i):
-        _, b, c, d = copies(i)
-        r = rows(i)
-        b.wait_recv()
-        mid[r] = (near_ref[1, r].astype(f32) + beside[r].astype(f32)).astype(jnp.bfloat16)
-
-        @pl.when(me + 2 < n)
-        def _():
-            c.wait_recv()
-            mid[r] = (
-                near_ref[1, r].astype(f32) + beside[r].astype(f32) + far_in[r].astype(f32)
-            ).astype(jnp.bfloat16)
-
-        pl.when(me >= 2)(d.start)
-
-    loop(send_mid)
-
-    def finish(i):
-        a, b, c, d = copies(i)
-        r = rows(i)
-        total_ref[r] = down_ref[r]
-
-        @pl.when(odd == 0)
-        def _():
-            a.wait_recv()
-            total_ref[r] = down_ref[r] + other[r].astype(f32)
-
-        @pl.when(me + 2 < n)
-        def _():
-            d.wait_recv()
-            total_ref[r] = total_ref[r] + mid_in[r].astype(f32)
-
-        a.wait_send()
-        b.wait_send()
-
-        @pl.when(me >= 2)
-        def _():
-            c.wait_send()
-            d.wait_send()
-
-    loop(finish)
-
-
-def give_back(n, near, down):
-    return pl.pallas_call(
-        functools.partial(give_back_kernel, n),
-        out_shape=jax.ShapeDtypeStruct(down.shape, jnp.float32),
-        in_specs=[VMEM] * 2,
-        out_specs=VMEM,
-        scratch_shapes=[pltpu.VMEM(down.shape, jnp.bfloat16)] * 6
-        + [pltpu.SemaphoreType.DMA((4, CUTS))] * 2,
-        compiler_params=pltpu.CompilerParams(
-            collective_id=2, has_side_effects=True, vmem_limit_bytes=40 * 1024 * 1024
-        ),
-    )(near, down)
-
-
-def head_sum_kernel(part_ref, out_ref, from_core, stage, from_y, send, recv):
-    h = lax.axis_index("head")
-    core, y = h % 2, h // 2
-    size = out_ref.shape[0] // CUTS
-    f32 = jnp.float32
-    mate = 2 * y + 1 - core
-    across = 2 * (1 - y) + core
-    barrier = pltpu.get_barrier_semaphore()
-    for peer in (mate, across):
-        pl.semaphore_signal(barrier, inc=1, device_id={"head": peer}, device_id_type=MESH)
-    pl.semaphore_wait(barrier, 2)
-
-    def rows(i):
-        return pl.ds(pl.multiple_of(i * size, size), size)
-
-    def to_head(source, dest, peer, kind, i):
-        return pltpu.make_async_remote_copy(
-            src_ref=source,
-            dst_ref=dest,
-            send_sem=send.at[kind, i],
-            recv_sem=recv.at[kind, i],
-            device_id={"head": peer},
-            device_id_type=MESH,
-        )
-
-    def copies(i):
-        r = rows(i)
-        return (
-            to_head(part_ref.at[2 * (1 - y) + 1 - core, r], from_core.at[0, r], mate, 0, i),
-            to_head(part_ref.at[2 * y + 1 - core, r], from_core.at[1, r], mate, 1, i),
-            to_head(stage.at[r], from_y.at[r], across, 2, i),
-        )
-
-    def loop(step):
-        lax.fori_loop(0, CUTS, lambda i, c: (step(i), c)[1], 0)
-
-    loop(lambda i: copies(i)[0].start())
-    loop(lambda i: copies(i)[1].start())
-
-    def pass_on(i):
-        a, _, c = copies(i)
-        r = rows(i)
-        a.wait_recv()
-        stage[r] = (
-            part_ref[2 * (1 - y) + core, r].astype(f32) + from_core[0, r].astype(f32)
-        ).astype(jnp.bfloat16)
-        c.start()
-
-    loop(pass_on)
-
-    def finish(i):
-        a, b, c = copies(i)
-        r = rows(i)
-        b.wait_recv()
-        c.wait_recv()
-        out_ref[r] = (
-            part_ref[2 * y + core, r].astype(f32)
-            + from_core[1, r].astype(f32)
-            + from_y[r].astype(f32)
-        ).astype(jnp.bfloat16)
-        a.wait_send()
-        b.wait_send()
-        c.wait_send()
-
-    loop(finish)
-
-
-def head_sum(parts):
-    block = parts.shape[1:]
-    return pl.pallas_call(
-        head_sum_kernel,
-        out_shape=jax.ShapeDtypeStruct(block, jnp.bfloat16),
-        in_specs=[VMEM],
-        out_specs=VMEM,
-        scratch_shapes=[
-            pltpu.VMEM((2,) + block, jnp.bfloat16),
-            pltpu.VMEM(block, jnp.bfloat16),
-            pltpu.VMEM(block, jnp.bfloat16),
-            pltpu.SemaphoreType.DMA((3, CUTS)),
-            pltpu.SemaphoreType.DMA((3, CUTS)),
-        ],
-        compiler_params=pltpu.CompilerParams(
-            collective_id=3, has_side_effects=True, vmem_limit_bytes=40 * 1024 * 1024
-        ),
-    )(parts)
-
-
 def swap_halves(x):
     half = x.shape[-1] // 2
     return jnp.concatenate([x[:, half:], x[:, :half]], axis=1)
@@ -507,28 +319,259 @@
     cot_ref[...] = (grad_ref[...].astype(jnp.float32) * factor).astype(jnp.bfloat16)
 
 
-def back_kernel(
-    total_ref, lin_ref, gain_ref, cos_ref, sin_ref, dq_ref, q_mat, kv_mat, out_ref, dkv
+def tail_kernel(
+    n,
+    near_ref,
+    down_ref,
+    lin_ref,
+    gain_ref,
+    cos_ref,
+    sin_ref,
+    dq_ref,
+    q_hbm,
+    kv_hbm,
+    out_ref,
+    q_mat,
+    kv_mat,
+    total,
+    part,
+    own,
+    beside,
+    other,
+    far_in,
+    far,
+    mid,
+    mid_in,
+    from_core,
+    stage,
+    from_y,
+    send,
+    recv,
+    hsend,
+    hrecv,
+    local,
 ):
+    me = lax.axis_index("seq")
+    odd = me % 2
+    pair = pair_of(me)
+    h = lax.axis_index("head")
+    core, y = h % 2, h // 2
+    mate = 2 * y + 1 - core
+    across = 2 * (1 - y) + core
+    size = near_ref.shape[1] // CUTS
     width = gain_ref.shape[1]
-    full = lin_ref.shape[1]
-    half = full // 2
-    for g in range(half // width):
-        cols = slice(g * width, (g + 1) * width)
-        dkv[:, cols] = rotate_back(
-            lin_ref[:, cols], gain_ref[...], cos_ref[...], sin_ref[...], total_ref[:, cols]
+    half = lin_ref.shape[1] // 2
+    f32 = jnp.float32
+    last = (((1,), (1,)), ((), ()))
+    q_copy = pltpu.make_async_copy(q_hbm, q_mat, local.at[0])
+    kv_copy = pltpu.make_async_copy(kv_hbm, kv_mat, local.at[1])
+    q_copy.start()
+    kv_copy.start()
+    barrier = pltpu.get_barrier_semaphore()
+    for peer in (mate, across):
+        pl.semaphore_signal(barrier, inc=1, device_id={"head": peer}, device_id_type=MESH)
+    greet_near(n, me, 2)
+
+    def rows(i):
+        return pl.ds(pl.multiple_of(i * size, size), size)
+
+    def to_head(source, dest, peer, kind, i):
+        return pltpu.make_async_remote_copy(
+            src_ref=source,
+            dst_ref=dest,
+            send_sem=hsend.at[kind, i],
+            recv_sem=hrecv.at[kind, i],
+            device_id={"head": peer},
+            device_id_type=MESH,
+        )
+
+    def other_copy(i):
+        r = rows(i)
+        return to_seq(near_ref.at[2 - 2 * odd, r], other.at[r], pair, send.at[0, i], recv.at[0, i])
+
+    def beside_copy(i):
+        r = rows(i)
+        return to_seq(near_ref.at[2 * odd, r], beside.at[r], pair, send.at[1, i], recv.at[1, i])
+
+    def far_copy(i):
+        r = rows(i)
+        return to_seq(far.at[r], far_in.at[r], me - 2, send.at[2, i], recv.at[2, i])
+
+    def mid_copy(i):
+        r = rows(i)
+        return to_seq(mid.at[r], mid_in.at[r], me - 2, send.at[3, i], recv.at[3, i])
+
+    pass_q, keep_q = 2 * (1 - y) + core, 2 * y + core
+    mate_pass_q, mate_keep_q = 2 * (1 - y) + 1 - core, 2 * y + 1 - core
+
+    def mate_pass_copy(i):
+        r = rows(i)
+        return to_head(part.at[mate_pass_q, r], from_core.at[0, r], mate, 0, i)
+
+    def mate_keep_copy(i):
+        r = rows(i)
+        return to_head(part.at[mate_keep_q, r], from_core.at[1, r], mate, 1, i)
+
+    def y_copy(i):
+        r = rows(i)
+        return to_head(stage.at[r], from_y.at[r], across, 2, i)
+
+    def loop(step):
+        lax.fori_loop(0, CUTS, lambda i, c: (step(i), c)[1], 0)
+
+    def begin(i):
+        other_copy(i).start()
+        beside_copy(i).start()
+
+    loop(begin)
+
+    def send_far(i):
+        r = rows(i)
+        far[r] = near_ref[3, r]
+
+        @pl.when(odd == 1)
+        def _():
+            other_copy(i).wait_recv()
+            far[r] = (near_ref[3, r].astype(f32) + other[r].astype(f32)).astype(jnp.bfloat16)
+
+        @pl.when(me >= 2)
+        def _():
+            far_copy(i).start()
+
+    loop(send_far)
+    q_copy.wait()
+
+    def quarter(k, carry):
+        total[k] = lax.dot_general(dq_ref[...], q_mat[k], last, preferred_element_type=f32)
+        return carry
+
+    lax.fori_loop(0, total.shape[0], quarter, 0)
+
+    def send_mid(i):
+        r = rows(i)
+        beside_copy(i).wait_recv()
+        mid[r] = (near_ref[1, r].astype(f32) + beside[r].astype(f32)).astype(jnp.bfloat16)
+
+        @pl.when(me + 2 < n)
+        def _():
+            far_copy(i).wait_recv()
+            mid[r] = (
+                near_ref[1, r].astype(f32) + beside[r].astype(f32) + far_in[r].astype(f32)
+            ).astype(jnp.bfloat16)
+
+        @pl.when(me >= 2)
+        def _():
+            mid_copy(i).start()
+
+    loop(send_mid)
+    kv_copy.wait()
+
+    def pass_on(i):
+        r = rows(i)
+        mate_pass_copy(i).wait_recv()
+        stage[r] = (part[pass_q, r].astype(f32) + from_core[0, r].astype(f32)).astype(jnp.bfloat16)
+        y_copy(i).start()
+
+    def middle(i):
+        r = rows(i)
+        own[r] = down_ref[r]
+
+        @pl.when(odd == 0)
+        def _():
+            other_copy(i).wait_recv()
+            own[r] = own[r] + other[r].astype(f32)
+
+        @pl.when(me + 2 < n)
+        def _():
+            mid_copy(i).wait_recv()
+            own[r] = own[r] + mid_in[r].astype(f32)
+
+        pieces = []
+        for g in range(half // width):
+            cols = slice(g * width, (g + 1) * width)
+            pieces.append(
+                rotate_back(
+                    lin_ref[r, cols], gain_ref[...], cos_ref[r], sin_ref[r], own[r, cols]
+                ).astype(jnp.bfloat16)
+            )
+        pieces.append(own[r, half:].astype(jnp.bfloat16))
+        dkv = jnp.concatenate(pieces, axis=1)
+
+        def product(k):
+            part[k, r] = (
+                total[k, r]
+                + lax.dot_general(dkv, kv_mat[k], last, preferred_element_type=f32)
+            ).astype(jnp.bfloat16)
+
+        product(mate_pass_q)
+        mate_pass_copy(i).start()
+        product(pass_q)
+        product(mate_keep_q)
+        mate_keep_copy(i).start()
+
+        @pl.when(i > 0)
+        def _():
+            pass_on(i - 1)
+
+        product(keep_q)
+
+    loop(middle)
+    pass_on(CUTS - 1)
+
+    def finish(i):
+        r = rows(i)
+        mate_keep_copy(i).wait_recv()
+        y_copy(i).wait_recv()
+        out_ref[r] = (
+            part[keep_q, r].astype(f32) + from_core[1, r].astype(f32) + from_y[r].astype(f32)
         ).astype(jnp.bfloat16)
-    dkv[:, half:] = total_ref[:, half:].astype(jnp.bfloat16)
-    last = (((1,), (1,)), ((), ()))
-
-    def quarter(i, carry):
-        out_ref[i] = (
-            lax.dot_general(dq_ref[...], q_mat[i], last, preferred_element_type=jnp.float32)
-            + lax.dot_general(dkv[...], kv_mat[i], last, preferred_element_type=jnp.float32)
-        ).astype(jnp.bfloat16)
-        return carry
-
-    lax.fori_loop(0, out_ref.shape[0], quarter, 0)
+        mate_pass_copy(i).wait_send()
+        mate_keep_copy(i).wait_send()
+        y_copy(i).wait_send()
+        other_copy(i).wait_send()
+        beside_copy(i).wait_send()
+
+        @pl.when(me >= 2)
+        def _():
+            far_copy(i).wait_send()
+            mid_copy(i).wait_send()
+
+    loop(finish)
+
+
+def tail(n, near, down, lin, gain, cosine, sine, dq, q_mat, kv_mat):
+    heads, wide, q_cols = q_mat.shape
+    tok_rows = lin.shape[0]
+    hbm = pl.BlockSpec(memory_space=pl.ANY)
+    bf16 = jnp.bfloat16
+    block = (tok_rows, wide)
+    return pl.pallas_call(
+        functools.partial(tail_kernel, n),
+        out_shape=jax.ShapeDtypeStruct(block, bf16),
+        in_specs=[VMEM] * 7 + [hbm] * 2,
+        out_specs=VMEM,
+        scratch_shapes=[
+            pltpu.VMEM(q_mat.shape, bf16),
+            pltpu.VMEM(kv_mat.shape, bf16),
+            pltpu.VMEM((heads,) + block, jnp.float32),
+            pltpu.VMEM((heads,) + block, bf16),
+            pltpu.VMEM(down.shape, jnp.float32),
+        ]
+        + [pltpu.VMEM(down.shape, bf16)] * 6
+        + [
+            pltpu.VMEM((2,) + block, bf16),
+            pltpu.VMEM(block, bf16),
+            pltpu.VMEM(block, bf16),
+            pltpu.SemaphoreType.DMA((4, CUTS)),
+            pltpu.SemaphoreType.DMA((4, CUTS)),
+            pltpu.SemaphoreType.DMA((3, CUTS)),
+            pltpu.SemaphoreType.DMA((3, CUTS)),
+            pltpu.SemaphoreType.DMA((2,)),
+        ],
+        compiler_params=pltpu.CompilerParams(
+            collective_id=2, has_side_effects=True, vmem_limit_bytes=48 * 1024 * 1024
+        ),
+    )(near, down, lin, gain, cosine, sine, dq, q_mat, kv_mat)
 
 
 def attend_kernel(
@@ -703,17 +746,11 @@
         ],
         compiler_params=ROOM,
     )(before, windows, q_lin, kv_own, near, cot, q_gain, cosine, sine)
-    total = give_back(n, dnear, down)
     heads = lax.axis_size("head")
-    parts = pl.pallas_call(
-        back_kernel,
-        out_shape=jax.ShapeDtypeStruct((heads, tok_rows, depth // heads), jnp.bfloat16),
-        in_specs=[VMEM] * 8,
-        out_specs=VMEM,
-        scratch_shapes=[pltpu.VMEM((tok_rows, kv_cols), jnp.bfloat16)],
-        compiler_params=ROOM,
-    )(
-        total,
+    grad_tokens = tail(
+        n,
+        dnear,
+        down,
         kv_lin,
         k_gain,
         cosine,
@@ -722,7 +759,6 @@
         q_full.reshape(heads, depth // heads, q_cols),
         kv_full.reshape(heads, depth // heads, kv_cols),
     )
-    grad_tokens = head_sum(parts)
     return (attended, grad_tokens)
 
 

time: 202 us -> 198 us (0.980); the launches traced: 199 us -> 197 us
  Pallas kernels: 183 us -> 180 us
    pallas_call x3 -> x1, Pallas kernels: 47.5 us -> 44.7 us  [tail(): pl.pallas_call(functools.partial(tail_kernel, n), out_shape=jax.ShapeDtyp...]
    unnamed x29 -> x31, local copies, waits for them, and re-layouts: 2.58 us -> 4.47 us
where the time goes in v3:
time: 198 us; the launch traced here: 197 us
  Pallas kernels  180 us (91%)
  matrix products  8.43 us (4%)
  local copies, waits for them, and re-layouts  5.84 us (3%)
  other arithmetic  2.15 us (1%)
    pallas_call x1, Pallas kernels, q_gather(): pl.pallas_call(functools.partial(q_gather_kernel, n), out_shape=[jax.Shap...  67.8 us
    pallas_call x1, Pallas kernels, kv_gather(): pl.pallas_call(functools.partial(kv_gather_kernel, n), out_shape=[jax.Sha...  55.8 us
    pallas_call x1, Pallas kernels, tail(): pl.pallas_call(functools.partial(tail_kernel, n), out_shape=jax.ShapeDtyp...  44.7 us
    pallas_call x1, Pallas kernels, body(): pl.pallas_call(functools.partial(attend_kernel, reach, kv_heads, scale),...  11.3 us
    unnamed x31, local copies, waits for them, and re-layouts  4.47 us
    dot_general x1, matrix products, body(): q_lin = jnp.dot(tokens, q_matrix, preferred_element_type=f32)  4.26 us
    dot_general x1, matrix products, body(): kv_lin = jnp.dot(tokens, kv_matrix, preferred_element_type=f32)  4.17 us

profile of v3, /device:TPU:18, one launch (start us, length us, event | category | flops | bytes accessed | tf_op | source)
XLA Modules:
  0.0 197.4 jit_solution(15460439157182475576)
XLA Ops:
  0.6 0.0 copy-start
  0.7 1.5 fusion.1
  2.1 1.2 broadcast_in_dim.14.tile_ref
  3.4 0.1 copy.16.kept_ref
  3.5 0.5 fusion
  4.1 0.1 pad_maximum_fusion
  4.2 0.0 copy-start.1
  4.2 0.0 copy-start.3
  4.2 55.8 %shard_map.113 = (bf16[8,672,512]{2,1,0:T(8,128)(2,1)}, f32[8,8,128]{2,1,0:T(8,128)}) custom-call(bf16[672,256]{1,0:T(8,128)(2,1)} %k_ref.1, bf16[672,256]{1,0:T(8,128)(2,1)} %v_ref.1, f32[8,128]{1,0:T(8,128)} %broadcast_in_dim.14.tile_ref), custom_call_target="tpu_custom_call" | custom-call | tf_op jit(solution)/shard_map/pallas_call | solution.py:181
  60.1 0.0 copy-done
  60.1 0.0 copy-start.10
  60.1 0.0 copy-start.11
  60.1 0.0 copy-start.12
  60.1 4.2 %convolution_bitcast_fusion.1.lin_ref = f32[256,512]{1,0:T(8,128)S(1)} fusion(bf16[256,5376]{1,0:T(8,128)(2,1)S(1)} %copy-done, bf16[5376,512]{1,0:T(8,128)(2,1)} %bitcast.18), kind=kOutput, calls=%fused_computation.1 | convolution fusion | flops 1409286144 | bytes 8781824 | tf_op jit(solution)/shard_map/dot_general | solution.py:718
  64.3 0.0 copy-done.10
  64.3 0.0 copy-done.11
  64.3 0.0 copy-done.12
  64.3 0.4 shard_map.114
  64.7 0.0 copy-start.5
  64.7 0.8 copy-done.5
  65.5 0.0 copy-start.8
  65.5 0.7 copy-done.8
  66.2 67.8 %shard_map.115 = (bf16[8,672,512]{2,1,0:T(8,128)(2,1)}, bf16[4,256,512]{2,1,0:T(8,128)(2,1)}) custom-call(bf16[672,512]{1,0:T(8,128)(2,1)} %q_ref.1, bf16[256,512]{1,0:T(8,128)(2,1)} %copy-done.8), custom_call_target="tpu_custom_call" | custom-call | tf_op jit(solution)/shard_map/pallas_call | solution.py:267
  134.0 0.0 copy-start.7
  134.1 0.0 copy-start.9
  134.1 0.0 copy-start.13
  134.1 0.0 copy-start.14
  134.1 0.0 copy-start.6
  134.1 4.3 %convolution_bitcast_fusion.lin_ref = f32[256,512]{1,0:T(8,128)S(1)} fusion(bf16[256,5376]{1,0:T(8,128)(2,1)S(1)} %copy-done, bf16[5376,512]{1,0:T(8,128)(2,1)} %bitcast.20), kind=kOutput, calls=%fused_computation | convolution fusion | flops 1409286144 | bytes 8781824 | tf_op jit(solution)/shard_map/dot_general | solution.py:731
  138.4 0.0 copy-done.1
  138.4 0.0 copy-done.3
  138.4 0.0 copy-done.7
  138.4 0.0 copy-done.9
  138.4 0.0 copy-done.13
  138.4 0.0 copy-done.14
  138.4 11.3 %shard_map.116 = (bf16[256,512]{1,0:T(8,128)(2,1)}, bf16[256,512]{1,0:T(8,128)(2,1)S(1)}, f32[256,512]{1,0:T(8,128)S(1)}, bf16[4,256,512]{2,1,0:T(8,128)(2,1)S(1)}) custom-call(s32[4]{0:T(128)S(1)} %compare_convert_fusion.there_ref, s32[4]{0:T(128)S(1)} %copy-done.13, f32[256,512]{1,0:T(8,128)S(1)} %convolution_bitcast_fusion.lin_ref, ...), custom_call_target="tpu_custom_call" | custom-call | tf_op jit(solution)/shard_map/pallas_call | solution.py:732
  149.7 0.0 copy-done.6
  149.7 0.0 copy-start.2
  149.7 0.9 copy-done.2
  150.6 0.0 copy-start.4
  150.6 0.9 copy-done.4
  151.5 44.7 %shard_map.117 = bf16[256,1344]{1,0:T(8,128)(2,1)S(1)} custom-call(bf16[4,256,512]{2,1,0:T(8,128)(2,1)S(1)} %get-tuple-element.19.near_ref, f32[256,512]{1,0:T(8,128)S(1)} %get-tuple-element.20.down_ref, f32[256,512]{1,0:T(8,128)S(1)} %copy-done.6, f32[1,128]{1,0:T(1,128)S(1)} %bitcast.16, f32[256,128]{1,0:T(8,128)S(1)} %copy-done.2, ...), custom_call_target="tpu_custom_call" | custom-call | tf_op jit(solution)/shard_map/pallas_call | solution.py:548
  196.3 1.1 copy.18
  (3 shorter events, 0.0 us)
Async XLA Ops:
  0.6 59.4 %copy-start = (bf16[256,5376]{1,0:T(8,128)(2,1)S(1)}, bf16[256,5376]{1,0:T(8,128)(2,1)}, u32[]{:S(2)}) copy-start(bf16[256,5376]{1,0:T(8,128)(2,1)} %param.10) | copy-start | bytes 8257540
  4.2 134.2 %copy-start.1 = (f32[256,128]{1,0:T(8,128)}, f32[256,128]{1,0:T(8,128)S(1)}, u32[]{:S(2)}) copy-start(f32[256,128]{1,0:T(8,128)S(1)} %get-tuple-element.31.cos_ref) | copy-start | bytes 393220
  4.2 134.2 %copy-start.3 = (f32[256,128]{1,0:T(8,128)}, f32[256,128]{1,0:T(8,128)S(1)}, u32[]{:S(2)}) copy-start(f32[256,128]{1,0:T(8,128)S(1)} %get-tuple-element.32.sin_ref) | copy-start | bytes 393220
  60.1 4.2 %copy-start.10 = (bf16[256,512]{1,0:T(8,128)(2,1)S(1)}, bf16[256,512]{1,0:T(8,128)(2,1)}, u32[]{:S(2)}) copy-start(bf16[256,512]{1,0:T(8,128)(2,1)} %grad_ref.1) | copy-start | bytes 786436
  60.1 4.2 %copy-start.11 = (f32[8,8,128]{2,1,0:T(8,128)S(1)}, f32[8,8,128]{2,1,0:T(8,128)}, u32[]{:S(2)}) copy-start(f32[8,8,128]{2,1,0:T(8,128)} %get-tuple-element.13.tiles_ref) | copy-start | bytes 98308
  60.1 4.2 %copy-start.12 = (f32[128]{0:T(128)S(1)}, f32[128]{0:T(128)}, u32[]{:S(2)}) copy-start(f32[128]{0:T(128)} %param.15) | copy-start | bytes 1540
  64.7 0.8 copy-start.5
  65.5 0.7 copy-start.8
  134.0 4.3 %copy-start.7 = (bf16[4,256,512]{2,1,0:T(8,128)(2,1)S(1)}, bf16[4,256,512]{2,1,0:T(8,128)(2,1)}, u32[]{:S(2)}) copy-start(bf16[4,256,512]{2,1,0:T(8,128)(2,1)} %get-tuple-element.16.near_ref) | copy-start | bytes 3145732
  134.1 4.3 %copy-start.9 = (bf16[256,512]{1,0:T(8,128)(2,1)S(1)}, bf16[256,512]{1,0:T(8,128)(2,1)}, u32[]{:S(2)}) copy-start(bf16[256,512]{1,0:T(8,128)(2,1)} %copy-done.8) | copy-start | bytes 786436
  134.1 4.3 %copy-start.13 = (s32[4]{0:T(128)S(1)}, s32[4]{0:T(128)}, u32[]{:S(2)}) copy-start(s32[4]{0:T(128)} %windows_ref.1) | copy-start | bytes 52
  134.1 4.3 %copy-start.14 = (f32[128]{0:T(128)S(1)}, f32[128]{0:T(128)}, u32[]{:S(2)}) copy-start(f32[128]{0:T(128)} %param.14) | copy-start | bytes 1540
  134.1 15.7 %copy-start.6 = (f32[256,512]{1,0:T(8,128)S(1)}, f32[256,512]{1,0:T(8,128)}, u32[]{:S(2)}) copy-start(f32[256,512]{1,0:T(8,128)} %copy-done.5) | copy-start | bytes 1572868
  149.7 0.9 copy-start.2
  150.6 0.9 copy-start.4

commit v4 on v3

--- a/solution.py
+++ b/solution.py
@@ -29,7 +29,7 @@
     return [(a, b - a) for a, b in zip(edges, edges[1:])]
 
 
-def ring_gather(n, jobs, me, send_sems, recv_sems, middle, later=None):
+def ring_gather(n, jobs, me, send_sems, recv_sems, middle, hooks=()):
     place = ring_place(me, n)
 
     def at(distance):
@@ -80,11 +80,12 @@
             copy(step, job).start()
         return carry
 
-    turn = n // 2 - 1
-    lax.fori_loop(1, turn, body, 0)
-    if later is not None:
-        later()
-    lax.fori_loop(turn, n - 1, body, 0)
+    done = 1
+    for turn, hook in hooks:
+        lax.fori_loop(done, turn, body, 0)
+        hook()
+        done = turn
+    lax.fori_loop(done, n - 1, body, 0)
     for job in range(len(jobs)):
         arrived(n - 2, job).wait_recv()
 
@@ -195,11 +196,15 @@
     )(k_weight, v_weight, tile)
 
 
-def q_gather_kernel(n, q_ref, kv_ref, q_out, near_out, send, recv, nsend, nrecv, local):
+def q_gather_kernel(n, q_ref, kv_ref, q_out, near_out, *sems):
+    greet_near(n, lax.axis_index("seq"))
+    q_and_near(n, q_ref, kv_ref, q_out, near_out, *sems)
+
+
+def q_and_near(n, q_ref, kv_ref, q_out, near_out, send, recv, nsend, nrecv, local, ready=None):
     me = lax.axis_index("seq")
     odd = me % 2
     rows = q_ref.shape[0]
-    greet_near(n, me)
     own = pltpu.make_async_copy(q_ref, q_out.at[me], local.at[0])
     pair = pair_of(me)
     up = to_seq(kv_ref, near_out.at[1], me + 2, nsend.at[0], nrecv.at[1])
@@ -219,12 +224,14 @@
             )
         )
 
-    pl.when(has_up)(up.start)
-    pl.when(odd == 0)(across.start)
-
     def middle():
         own.start()
-
+        if ready is not None:
+            ready()
+        pl.when(has_up)(up.start)
+        pl.when(odd == 0)(across.start)
+
+    def soon():
         @pl.when(me >= 2)
         def _():
             up.wait_recv()
@@ -237,7 +244,7 @@
             up_again.wait_recv()
             pl.when(odd == 1)(across_four.start)
 
-    ring_gather(n, jobs, me, send, recv, middle, later)
+    ring_gather(n, jobs, me, send, recv, middle, ((2, soon), (4, later)))
     own.wait()
 
     @pl.when(has_up)
@@ -317,6 +324,122 @@
     normalizer = jnp.sum(tiles_ref[...], axis=0)[0:1, 0:1]
     factor = kept_ref[...] * (tokens_total / normalizer)
     cot_ref[...] = (grad_ref[...].astype(jnp.float32) * factor).astype(jnp.bfloat16)
+
+
+def front_kernel(
+    n,
+    tokens_total,
+    k_ref,
+    v_ref,
+    tile_ref,
+    q_ref,
+    tokens_ref,
+    gain_ref,
+    cos_ref,
+    sin_ref,
+    kept_ref,
+    grad_ref,
+    kv_out,
+    q_out,
+    near_out,
+    lin_ref,
+    own_ref,
+    cot_ref,
+    tiles,
+    ksend,
+    krecv,
+    klocal,
+    *sems,
+):
+    me = lax.axis_index("seq")
+    rows, width = k_ref.shape
+    greet_near(n, me)
+
+    def block(owner, a=0, size=rows):
+        return pl.ds(pl.multiple_of(owner * rows + a, 16), size)
+
+    own = [
+        pltpu.make_async_copy(k_ref, kv_out.at[block(me), pl.ds(0, width)], klocal.at[0]),
+        pltpu.make_async_copy(v_ref, kv_out.at[block(me), pl.ds(width, width)], klocal.at[1]),
+        pltpu.make_async_copy(tile_ref, tiles.at[me], klocal.at[2]),
+    ]
+    jobs = []
+    for a, size in row_cuts(rows, 2):
+        for ref, col, way in ((k_ref, 0, 1), (v_ref, width, -1)):
+            jobs.append(
+                (
+                    ref.at[pl.ds(a, size)],
+                    lambda owner, a=a, size=size, col=col: kv_out.at[
+                        block(owner, a, size), pl.ds(col, width)
+                    ],
+                    way,
+                )
+            )
+    jobs.append((tile_ref, lambda owner: tiles.at[owner], 1))
+
+    def begin():
+        for c in own:
+            c.start()
+
+    ring_gather(n, jobs, me, ksend, krecv, begin)
+    for c in own:
+        c.wait()
+    step = 384
+
+    def ready():
+        lin_ref[...] = jnp.zeros_like(lin_ref)
+
+        def product(i, carry):
+            part = pl.ds(pl.multiple_of(i * step, step), step)
+            lin_ref[...] += jnp.dot(
+                tokens_ref[:, part], kv_out[part, :], preferred_element_type=jnp.float32
+            )
+            return carry
+
+        lax.fori_loop(0, n * rows // step, product, 0)
+        kv_ready_kernel(
+            tokens_total, lin_ref, gain_ref, cos_ref, sin_ref, tiles, kept_ref, grad_ref, own_ref, cot_ref
+        )
+
+    q_and_near(n, q_ref, own_ref, q_out, near_out, *sems, ready=ready)
+
+
+def front(n, reach, k_weight, v_weight, tile, q_weight, tokens, gain, cosine, sine, kept, grad):
+    rows, width = k_weight.shape
+    q_cols = q_weight.shape[1]
+    tok_rows = tokens.shape[0]
+    kv_jobs = 2 * len(row_cuts(rows, 2)) + 1
+    q_jobs = len(row_cuts(rows, 4))
+    hbm = pl.BlockSpec(memory_space=pl.ANY)
+    bf16 = jnp.bfloat16
+    dma = pltpu.SemaphoreType.DMA
+    return pl.pallas_call(
+        functools.partial(front_kernel, n, float(tok_rows * n)),
+        out_shape=[
+            jax.ShapeDtypeStruct((n * rows, 2 * width), bf16),
+            jax.ShapeDtypeStruct((n, rows, q_cols), bf16),
+            jax.ShapeDtypeStruct((reach, tok_rows, 2 * width), bf16),
+            jax.ShapeDtypeStruct((tok_rows, 2 * width), jnp.float32),
+            jax.ShapeDtypeStruct((tok_rows, 2 * width), bf16),
+            jax.ShapeDtypeStruct((tok_rows, q_cols), bf16),
+        ],
+        in_specs=[hbm] * 2 + [VMEM, hbm] + [VMEM] * 6,
+        out_specs=[VMEM, hbm, hbm] + [VMEM] * 3,
+        scratch_shapes=[
+            pltpu.VMEM((n,) + tile.shape, jnp.float32),
+            dma((n - 1, kv_jobs)),
+            dma((n - 1, kv_jobs)),
+            dma((3,)),
+            dma((n - 1, q_jobs)),
+            dma((n - 1, q_jobs)),
+            dma((5,)),
+            dma((reach,)),
+            dma((1,)),
+        ],
+        compiler_params=pltpu.CompilerParams(
+            collective_id=0, has_side_effects=True, vmem_limit_bytes=40 * 1024 * 1024
+        ),
+    )(k_weight, v_weight, tile, q_weight, tokens, gain, cosine, sine, kept, grad)
 
 
 def tail_kernel(
@@ -701,7 +824,6 @@
 
     kept = token_weight * loss_mask.astype(f32)
     tile = jnp.broadcast_to(jnp.sum(kept), (8, 128))
-    kv_full, tiles = kv_gather(n, k_weight, v_weight, tile)
     positions = me * tok_rows + jnp.arange(tok_rows, dtype=jnp.int32)
     half_width = head_width // 2
     frequency = 10000.0 ** (-(jnp.arange(half_width, dtype=f32) * 2.0) / head_width)
@@ -714,19 +836,36 @@
     q_gain = q_gain[None, :]
     k_gain = k_gain[None, :]
 
-    kv_matrix = kv_full.reshape(depth, kv_cols)
-    kv_lin = jnp.dot(tokens, kv_matrix, preferred_element_type=f32)
-    kv_own, cot = pl.pallas_call(
-        functools.partial(kv_ready_kernel, float(tok_rows * n)),
-        out_shape=[
-            jax.ShapeDtypeStruct((tok_rows, kv_cols), jnp.bfloat16),
-            jax.ShapeDtypeStruct((tok_rows, q_cols), jnp.bfloat16),
-        ],
-        in_specs=[VMEM] * 7,
-        out_specs=[VMEM] * 2,
-        compiler_params=ROOM,
-    )(kv_lin, k_gain, cosine, sine, tiles, kept[:, None], grad_attn)
-    q_full, near = q_gather(n, reach, q_weight, kv_own)
+    if k_weight.shape[0] % 16 == 0 and depth % 384 == 0:
+        kv_full, q_full, near, kv_lin, kv_own, cot = front(
+            n,
+            reach,
+            k_weight,
+            v_weight,
+            tile,
+            q_weight,
+            tokens,
+            k_gain,
+            cosine,
+            sine,
+            kept[:, None],
+            grad_attn,
+        )
+    else:
+        kv_full, tiles = kv_gather(n, k_weight, v_weight, tile)
+        kv_matrix = kv_full.reshape(depth, kv_cols)
+        kv_lin = jnp.dot(tokens, kv_matrix, preferred_element_type=f32)
+        kv_own, cot = pl.pallas_call(
+            functools.partial(kv_ready_kernel, float(tok_rows * n)),
+            out_shape=[
+                jax.ShapeDtypeStruct((tok_rows, kv_cols), jnp.bfloat16),
+                jax.ShapeDtypeStruct((tok_rows, q_cols), jnp.bfloat16),
+            ],
+            in_specs=[VMEM] * 7,
+            out_specs=[VMEM] * 2,
+            compiler_params=ROOM,
+        )(kv_lin, k_gain, cosine, sine, tiles, kept[:, None], grad_attn)
+        q_full, near = q_gather(n, reach, q_weight, kv_own)
     q_matrix = q_full.reshape(depth, q_cols)
     q_lin = jnp.dot(tokens, q_matrix, preferred_element_type=f32)
     attended, dq_lin, down, dnear = pl.pallas_call(

time: 198 us -> 196 us (0.990)
  local copies, waits for them, and re-layouts: 5.84 us -> 8.35 us
  matrix products: 8.43 us -> 6.13 us
  Pallas kernels: 180 us -> 178 us
    dot_general x1 -> x0, matrix products: 4.17 us -> none  [body(): kv_lin = jnp.dot(tokens, kv_matrix, preferred_element_type=f32)]
    unnamed x31 -> x21, local copies, waits for them, and re-layouts: 4.47 us -> 7.57 us
    pallas_call x3 -> x1, Pallas kernels: 124 us -> 123 us  [front(): pl.pallas_call(functools.partial(front_kernel, n, float(tok_rows * n)), o...]
where the time goes in v4:
time: 196 us; the launch traced here: 195 us
  Pallas kernels  178 us (91%)
  local copies, waits for them, and re-layouts  8.35 us (4%)
  matrix products  6.13 us (3%)
  other arithmetic  2 us (1%)
    pallas_call x1, Pallas kernels, front(): pl.pallas_call(functools.partial(front_kernel, n, float(tok_rows * n)), o...  123 us
    pallas_call x1, Pallas kernels, tail(): pl.pallas_call(functools.partial(tail_kernel, n), out_shape=jax.ShapeDtyp...  43.9 us
    pallas_call x1, Pallas kernels, body(): pl.pallas_call(functools.partial(attend_kernel, reach, kv_heads, scale),...  11.3 us
    unnamed x21, local copies, waits for them, and re-layouts  7.57 us
    dot_general x1, matrix products, body(): q_lin = jnp.dot(tokens, q_matrix, preferred_element_type=f32)  6.13 us

profile of v4, /device:TPU:18, one launch (start us, length us, event | category | flops | bytes accessed | tf_op | source)
XLA Modules:
  0.0 195.3 jit_solution(5074969686429735908)
XLA Ops:
  0.7 1.3 fusion.1
  2.0 0.6 broadcast_in_dim.14.tile_ref
  2.6 0.1 copy.14.kept_ref
  2.8 0.5 fusion
  3.3 0.1 pad_maximum_fusion
  3.5 0.0 copy-start.1
  3.5 1.8 copy-done.1
  5.2 0.0 copy-start.2
  5.2 1.1 copy-done.2
  6.3 0.0 copy-start.3
  6.3 1.0 copy-done.3
  7.3 0.0 copy-start.4
  7.3 1.0 copy-done.4
  8.3 0.0 copy-start.5
  8.3 0.9 copy-done.5
  9.2 0.0 copy-start.6
  9.3 0.7 copy-done.6
  9.9 122.8 %shard_map.113 = (bf16[5376,512]{1,0:T(8,128)(2,1)S(1)}, bf16[8,672,512]{2,1,0:T(8,128)(2,1)}, bf16[4,256,512]{2,1,0:T(8,128)(2,1)S(1)}, f32[256,512]{1,0:T(8,12...) custom-call(bf16[672,256]{1,0:T(8,128)(2,1)S(1)} %copy-done.3, bf16[672,256]{1,0:T(8,128)(2,1)S(1)} %copy-done.4, ...), custom_call_target="tpu_custom_call" | custom-call | tf_op jit(solution)/shard_map/pallas_call | solution.py:416
  132.8 0.0 copy-start
  132.8 0.0 copy-start.8
  132.8 0.0 copy-start.9
  132.8 0.0 copy-start.7
  132.8 6.1 %convolution_bitcast_fusion.lin_ref = f32[256,512]{1,0:T(8,128)S(1)} fusion(bf16[256,5376]{1,0:T(8,128)(2,1)S(1)} %copy-done.1, bf16[5376,512]{1,0:T(8,128)(2,1)} %bitcast.14), kind=kOutput, calls=%fused_computation | convolution fusion | flops 1409286144 | bytes 8781824 | tf_op jit(solution)/shard_map/dot_general | solution.py:870
  138.9 0.0 copy-done
  139.0 0.0 copy-done.8
  139.0 0.0 copy-done.9
  139.0 11.3 %shard_map.114 = (bf16[256,512]{1,0:T(8,128)(2,1)}, bf16[256,512]{1,0:T(8,128)(2,1)S(1)}, f32[256,512]{1,0:T(8,128)S(1)}, bf16[4,256,512]{2,1,0:T(8,128)(2,1)S(1)}) custom-call(s32[4]{0:T(128)S(1)} %compare_convert_fusion.there_ref, s32[4]{0:T(128)S(1)} %copy-done.8, f32[256,512]{1,0:T(8,128)S(1)} %convolution_bitcast_fusion.lin_ref, ...), custom_call_target="tpu_custom_call" | custom-call | tf_op jit(solution)/shard_map/pallas_call | solution.py:871
  150.3 0.0 copy-done.7
  150.3 43.9 %shard_map.115 = bf16[256,1344]{1,0:T(8,128)(2,1)S(1)} custom-call(bf16[4,256,512]{2,1,0:T(8,128)(2,1)S(1)} %get-tuple-element.17.near_ref, f32[256,512]{1,0:T(8,128)S(1)} %get-tuple-element.18.down_ref, f32[256,512]{1,0:T(8,128)S(1)} %get-tuple-element.19.lin_ref, f32[1,128]{1,0:T(1,128)S(1)} %bitcast.12, f32[256,128]{1,0:T(8,128)S(1)} %get-tuple-element.31.cos_ref, ...), custom_call_target="tpu_custom_call" | custom-call | tf_op jit(solution)/shard_map/pallas_call | solution.py:671
  194.2 1.1 copy.16
  (3 shorter events, 0.0 us)
Async XLA Ops:
  3.5 1.8 copy-start.1
  5.2 1.1 copy-start.2
  6.3 1.0 copy-start.3
  7.3 1.0 copy-start.4
  8.3 0.9 copy-start.5
  9.2 0.7 copy-start.6
  132.8 6.2 %copy-start = (bf16[5376,512]{1,0:T(8,128)(2,1)}, bf16[5376,512]{1,0:T(8,128)(2,1)S(1)}, u32[]{:S(2)}) copy-start(bf16[5376,512]{1,0:T(8,128)(2,1)S(1)} %get-tuple-element.21) | copy-start | bytes 16515076
  132.8 6.2 %copy-start.8 = (s32[4]{0:T(128)S(1)}, s32[4]{0:T(128)}, u32[]{:S(2)}) copy-start(s32[4]{0:T(128)} %windows_ref.1) | copy-start | bytes 52
  132.8 6.2 %copy-start.9 = (f32[128]{0:T(128)S(1)}, f32[128]{0:T(128)}, u32[]{:S(2)}) copy-start(f32[128]{0:T(128)} %param.14) | copy-start | bytes 1540
  132.8 17.5 %copy-start.7 = (f32[128]{0:T(128)S(1)}, f32[128]{0:T(128)}, u32[]{:S(2)}) copy-start(f32[128]{0:T(128)} %param.15) | copy-start | bytes 1540

commit v5 on v4

--- a/solution.py
+++ b/solution.py
@@ -333,12 +333,12 @@
     v_ref,
     tile_ref,
     q_ref,
-    tokens_ref,
+    tokens_hbm,
     gain_ref,
-    cos_ref,
-    sin_ref,
+    cos_hbm,
+    sin_hbm,
     kept_ref,
-    grad_ref,
+    grad_hbm,
     kv_out,
     q_out,
     near_out,
@@ -346,6 +346,10 @@
     own_ref,
     cot_ref,
     tiles,
+    tokens_ref,
+    cos_ref,
+    sin_ref,
+    grad_ref,
     ksend,
     krecv,
     klocal,
@@ -362,6 +366,10 @@
         pltpu.make_async_copy(k_ref, kv_out.at[block(me), pl.ds(0, width)], klocal.at[0]),
         pltpu.make_async_copy(v_ref, kv_out.at[block(me), pl.ds(width, width)], klocal.at[1]),
         pltpu.make_async_copy(tile_ref, tiles.at[me], klocal.at[2]),
+        pltpu.make_async_copy(tokens_hbm, tokens_ref, klocal.at[3]),
+        pltpu.make_async_copy(cos_hbm, cos_ref, klocal.at[4]),
+        pltpu.make_async_copy(sin_hbm, sin_ref, klocal.at[5]),
+        pltpu.make_async_copy(grad_hbm, grad_ref, klocal.at[6]),
     ]
     jobs = []
     for a, size in row_cuts(rows, 2):
@@ -423,13 +431,17 @@
             jax.ShapeDtypeStruct((tok_rows, 2 * width), bf16),
             jax.ShapeDtypeStruct((tok_rows, q_cols), bf16),
         ],
-        in_specs=[hbm] * 2 + [VMEM, hbm] + [VMEM] * 6,
+        in_specs=[hbm] * 2 + [VMEM, hbm, hbm, VMEM, hbm, hbm, VMEM, hbm],
         out_specs=[VMEM, hbm, hbm] + [VMEM] * 3,
         scratch_shapes=[
             pltpu.VMEM((n,) + tile.shape, jnp.float32),
+            pltpu.VMEM(tokens.shape, bf16),
+            pltpu.VMEM(cosine.shape, jnp.float32),
+            pltpu.VMEM(sine.shape, jnp.float32),
+            pltpu.VMEM(grad.shape, bf16),
             dma((n - 1, kv_jobs)),
             dma((n - 1, kv_jobs)),
-            dma((3,)),
+            dma((7,)),
             dma((n - 1, q_jobs)),
             dma((n - 1, q_jobs)),
             dma((5,)),

time: 196 us -> 196 us (level)
  no operation moved by 1% of the time
where the time goes in v5:
time: 196 us; the launch traced here: 195 us
  Pallas kernels  178 us (91%)
  local copies, waits for them, and re-layouts  8.35 us (4%)
  matrix products  6.13 us (3%)
  other arithmetic  2 us (1%)
    pallas_call x1, Pallas kernels, front(): pl.pallas_call(functools.partial(front_kernel, n, float(tok_rows * n)), o...  123 us
    pallas_call x1, Pallas kernels, tail(): pl.pallas_call(functools.partial(tail_kernel, n), out_shape=jax.ShapeDtyp...  44 us
    pallas_call x1, Pallas kernels, body(): pl.pallas_call(functools.partial(attend_kernel, reach, kv_heads, scale),...  11.3 us
    unnamed x21, local copies, waits for them, and re-layouts  7.57 us
    dot_general x1, matrix products, body(): q_lin = jnp.dot(tokens, q_matrix, preferred_element_type=f32)  6.13 us

profile of v5, /device:TPU:18, one launch (start us, length us, event | category | flops | bytes accessed | tf_op | source)
XLA Modules:
  0.0 195.4 jit_solution(15470239613672351022)
XLA Ops:
  0.7 1.3 fusion.1
  2.0 0.6 broadcast_in_dim.14.tile_ref
  2.6 0.1 copy.14.kept_ref
  2.8 0.5 fusion
  3.3 0.1 pad_maximum_fusion
  3.5 0.0 copy-start.1
  3.5 1.8 copy-done.1
  5.2 0.0 copy-start.2
  5.2 1.1 copy-done.2
  6.3 0.0 copy-start.3
  6.3 1.0 copy-done.3
  7.3 0.0 copy-start.4
  7.3 1.0 copy-done.4
  8.3 0.0 copy-start.5
  8.3 0.9 copy-done.5
  9.2 0.0 copy-start.6
  9.3 0.7 copy-done.6
  9.9 122.9 %shard_map.113 = (bf16[5376,512]{1,0:T(8,128)(2,1)S(1)}, bf16[8,672,512]{2,1,0:T(8,128)(2,1)}, bf16[4,256,512]{2,1,0:T(8,128)(2,1)S(1)}, f32[256,512]{1,0:T(8,12...) custom-call(bf16[672,256]{1,0:T(8,128)(2,1)S(1)} %copy-done.3, bf16[672,256]{1,0:T(8,128)(2,1)S(1)} %copy-done.4, ...), custom_call_target="tpu_custom_call" | custom-call | tf_op jit(solution)/shard_map/pallas_call | solution.py:424
  132.8 0.0 copy-start
  132.8 0.0 copy-start.8
  132.8 0.0 copy-start.9
  132.8 0.0 copy-start.7
  132.8 6.1 %convolution_bitcast_fusion.lin_ref = f32[256,512]{1,0:T(8,128)S(1)} fusion(bf16[256,5376]{1,0:T(8,128)(2,1)S(1)} %copy-done.1, bf16[5376,512]{1,0:T(8,128)(2,1)} %bitcast.14), kind=kOutput, calls=%fused_computation | convolution fusion | flops 1409286144 | bytes 8781824 | tf_op jit(solution)/shard_map/dot_general | solution.py:882
  139.0 0.0 copy-done
  139.0 0.0 copy-done.8
  139.0 0.0 copy-done.9
  139.0 11.3 %shard_map.114 = (bf16[256,512]{1,0:T(8,128)(2,1)}, bf16[256,512]{1,0:T(8,128)(2,1)S(1)}, f32[256,512]{1,0:T(8,128)S(1)}, bf16[4,256,512]{2,1,0:T(8,128)(2,1)S(1)}) custom-call(s32[4]{0:T(128)S(1)} %compare_convert_fusion.there_ref, s32[4]{0:T(128)S(1)} %copy-done.8, f32[256,512]{1,0:T(8,128)S(1)} %convolution_bitcast_fusion.lin_ref, ...), custom_call_target="tpu_custom_call" | custom-call | tf_op jit(solution)/shard_map/pallas_call | solution.py:883
  150.3 0.0 copy-done.7
  150.3 44.0 %shard_map.115 = bf16[256,1344]{1,0:T(8,128)(2,1)S(1)} custom-call(bf16[4,256,512]{2,1,0:T(8,128)(2,1)S(1)} %get-tuple-element.17.near_ref, f32[256,512]{1,0:T(8,128)S(1)} %get-tuple-element.18.down_ref, f32[256,512]{1,0:T(8,128)S(1)} %get-tuple-element.19.lin_ref, f32[1,128]{1,0:T(1,128)S(1)} %bitcast.12, f32[256,128]{1,0:T(8,128)S(1)} %get-tuple-element.31.cos_hbm.cos_ref, ...), custom_call_target="tpu_custom_call" | custom-call | tf_op jit(solution)/shard_map/pallas_call | solution.py:683
  194.3 1.1 copy.16
  (3 shorter events, 0.0 us)
Async XLA Ops:
  3.5 1.8 copy-start.1
  5.2 1.1 copy-start.2
  6.3 1.0 copy-start.3
  7.3 1.0 copy-start.4
  8.3 0.9 copy-start.5
  9.2 0.7 copy-start.6
  132.8 6.2 %copy-start = (bf16[5376,512]{1,0:T(8,128)(2,1)}, bf16[5376,512]{1,0:T(8,128)(2,1)S(1)}, u32[]{:S(2)}) copy-start(bf16[5376,512]{1,0:T(8,128)(2,1)S(1)} %get-tuple-element.21) | copy-start | bytes 16515076
  132.8 6.2 %copy-start.8 = (s32[4]{0:T(128)S(1)}, s32[4]{0:T(128)}, u32[]{:S(2)}) copy-start(s32[4]{0:T(128)} %windows_ref.1) | copy-start | bytes 52
  132.8 6.2 %copy-start.9 = (f32[128]{0:T(128)S(1)}, f32[128]{0:T(128)}, u32[]{:S(2)}) copy-start(f32[128]{0:T(128)} %param.14) | copy-start | bytes 1540
  132.8 17.5 %copy-start.7 = (f32[128]{0:T(128)S(1)}, f32[128]{0:T(128)}, u32[]{:S(2)}) copy-start(f32[128]{0:T(128)} %param.15) | copy-start | bytes 1540
